TPU v7x, 512 devices: a whole 4x4x16 slice. The times are simulated.
512 devices in a mesh: fam: 8 (over y, core), depth: 64 (over x, z).
Axes of the slice: x: 4, y: 4, z: 16, core: 2. Of those that a mesh axis runs over, the one named last changes fastest.
Arguments:
- embedded_homologs: bfloat16 [1024, 256, 768], P(('fam', 'depth')), parts along dimension 0
- normalizer_scale: float32 [768], replicated, may hold values from 0.5 to 1.5
- probe_projector: bfloat16 [768, 768], P('depth')
- lookup_projector: bfloat16 [768, 768], P('depth')
- content_projector: bfloat16 [768, 768], P('depth'), may hold values from -0.21875 to 0.21875
- final_projector: bfloat16 [768, 768], P('depth'), may hold values from -0.21875 to 0.21875
- live_member_tally: int32 [512], P(('fam', 'depth')), parts along dimension 0, may hold values from 1 to 2, 96 in all
Outputs:
- mixed: bfloat16 [1024, 256, 768], P(('fam', 'depth')), parts along dimension 0
There are 8 independent parts, one for each index of `fam`. A program takes and returns all parts, laid end to end along the dimension named above; an argument that names none is the same for every part. Nothing has to cross between parts.
Inputs may be any that keep to these rules, and one draw needn't show every extreme that they name: Device d's live rows are its first live_member_tally[d] slots; one device of each family has all 2 slots live.
All inputs are finite; a program needn't handle non-finite values.
Results may differ from a plain program's by a relative error of at most 0.009.
Values may be sent and summed in bfloat16 or wider, within the bound.
No kernel may reach another device: no remote copies, remote signals or barrier semaphores. Data moves between devices by JAX's collectives and lax.ppermute only.
A program may use at most 64 MiB of HBM per device.

v0:
```python
import math

import jax
import jax.numpy as jnp
from jax import lax
from jax.sharding import PartitionSpec as P

HEADS = 12


def per_device(
    embedded_homologs,
    normalizer_scale,
    probe_projector,
    lookup_projector,
    content_projector,
    final_projector,
    live_member_tally,
):
    reserved_places, residue_positions, embedding_dimension = embedded_homologs.shape
    head_size = embedding_dimension // HEADS
    incoming_features = embedded_homologs.astype(jnp.float32)
    mean = jnp.mean(incoming_features, axis=-1, keepdims=True)
    var = jnp.mean((incoming_features - mean) ** 2, axis=-1, keepdims=True)
    normed = ((incoming_features - mean) / jnp.sqrt(var + 1e-05) * normalizer_scale).astype(
        jnp.bfloat16
    )
    flat = normed.reshape(reserved_places * residue_positions, embedding_dimension)
    live = (jnp.arange(reserved_places) < live_member_tally[0]).astype(jnp.float32)
    count = live_member_tally[0].astype(jnp.float32)
    pieces = (
        lax.all_gather(probe_projector, "depth", axis=0, tiled=True),
        lax.all_gather(lookup_projector, "depth", axis=0, tiled=True),
        lax.all_gather(content_projector, "depth", axis=0, tiled=True),
    )
    features = flat
    query, keys, value = tuple(
        (jnp.dot(features, piece, preferred_element_type=jnp.float32) for piece in pieces)
    )
    query = (
        query.reshape(reserved_places, residue_positions, embedding_dimension) * live[:, None, None]
    ).astype(jnp.bfloat16)
    query = query.reshape(reserved_places, residue_positions, HEADS, head_size)
    keys = keys.astype(jnp.bfloat16).reshape(reserved_places, residue_positions, HEADS, head_size)
    value = value.astype(jnp.bfloat16).reshape(reserved_places, residue_positions, HEADS, head_size)
    partial_logits = jnp.einsum("rihe,rjhe->hij", query, keys, preferred_element_type=jnp.float32)
    summed, depth = lax.psum((partial_logits, count), "depth")
    logits = summed / (math.sqrt(head_size) * jnp.sqrt(depth))
    probs = jax.nn.softmax(logits, axis=-1).astype(jnp.bfloat16)
    context = jnp.einsum("hij,rjhe->rihe", probs, value, preferred_element_type=jnp.float32).astype(
        jnp.bfloat16
    )
    context = context.reshape(reserved_places * residue_positions, embedding_dimension)
    features = context
    mixed = jnp.dot(
        features,
        lax.all_gather(final_projector, "depth", axis=0, tiled=True),
        preferred_element_type=jnp.float32,
    )
    return (
        mixed.reshape(reserved_places, residue_positions, embedding_dimension) * live[:, None, None]
    ).astype(jnp.bfloat16)


def solution(mesh):
    return jax.shard_map(
        per_device,
        mesh=mesh,
        in_specs=(
            P(("fam", "depth"), None, None),
            P(),
            P("depth", None),
            P("depth", None),
            P("depth", None),
            P("depth", None),
            P(("fam", "depth")),
        ),
        out_specs=P(("fam", "depth"), None, None),
        check_vma=False,
    )
```

profile of v0, /device:TPU:8, one launch (start us, length us, event | category | flops | bytes accessed | tf_op | source)
XLA Modules:
  0.0 875.5 jit_solution(13174906317581897411)
XLA Ops:
  6.5 0.7 all-gather.11.cloned.1.call-update
  7.3 0.7 all-gather.13.cloned.1.call-update
  8.1 0.7 all-gather.9.cloned.1.call-update
  10.0 1.3 convert_reduce_fusion
  11.3 1.5 fusion.3
  13.2 142.0 %all-gather.11.cloned.1.call-done = bf16[64,12,768]{2,1,0:T(8,128)(2,1)} async-done(((bf16[1,12,768]{2,1,0:T(8,128)(2,1)}), bf16[64,12,768]{2,1,0:T(8,128)(2,1)}) %all-gather.11.cloned.1.call-update) | async-done | bytes 1179664 | tf_op jit(solution)/shard_map/all_gather | solution.py:32
  155.2 2.2 reshape.51
  157.4 1.7 multiply_convert_fusion.1
  159.1 1.4 copy.20
  160.5 133.9 %all-gather.13.cloned.1.call-done = bf16[64,12,768]{2,1,0:T(8,128)(2,1)} async-done(((bf16[1,12,768]{2,1,0:T(8,128)(2,1)}), bf16[64,12,768]{2,1,0:T(8,128)(2,1)}) %all-gather.13.cloned.1.call-update) | async-done | bytes 1179664 | tf_op jit(solution)/shard_map/all_gather | solution.py:33
  294.4 2.2 reshape.48
  296.6 1.7 convolution_convert_fusion
  298.3 1.4 copy.21
  299.9 2.3 convolution_bitcast_fusion
  302.2 142.0 %psum.15 = f32[]{:T(128)} all-reduce(f32[]{:T(128)S(6)} %convert_element_type.43), channel_id=1, replica_groups=mesh['fam'=8,'depth'=64] {'depth'}, use_global_device_ids=true, to_apply=%region_3.0 | all-reduce | flops 1 | bytes 8 | tf_op jit(solution)/shard_map/psum | solution.py:47
  445.0 2.3 reshape.44
  447.3 1.7 convolution_convert_fusion.1
  448.9 1.4 copy.19
  450.5 122.2 %all-gather.15.cloned.1.call-done = bf16[64,12,768]{2,1,0:T(8,128)(2,1)} async-done(((bf16[1,12,768]{2,1,0:T(8,128)(2,1)}), bf16[64,12,768]{2,1,0:T(8,128)(2,1)}) %all-gather.15.cloned.1.call-update) | async-done | bytes 1179664 | tf_op jit(solution)/shard_map/all_gather | solution.py:57
  572.7 2.2 reshape.54
  574.9 282.0 %all-reduce.2.cloned.1.call-done = f32[12,256,256]{2,1,0:T(8,128)} async-done(((f32[12,256,256]{2,1,0:T(8,128)}), f32[12,256,256]{2,1,0:T(8,128)}) %all-reduce.2.cloned.1.call-update) | async-done | bytes 3145744 | tf_op jit(solution)/shard_map/psum | solution.py:47
  856.9 2.8 fusion.18
  859.8 7.4 fusion.11
  867.3 1.7 multiply_convert_fusion
  (19 shorter events, 1.5 us)
Async XLA Ops:
  6.5 6.3 copy-start
  6.5 6.3 copy-start.1
  6.5 148.6 %all-gather.11.cloned.1.call-start = ((), (), s32[]{:S(2)}) async-start(), calls=%async_computation.2 | async-start | bytes 1597440 | tf_op jit(solution)/shard_map/all_gather | solution.py:32
  7.3 287.1 %all-gather.13.cloned.1.call-start = ((), (), s32[]{:S(2)}) async-start(), calls=%async_computation.3 | async-start | bytes 1597440 | tf_op jit(solution)/shard_map/all_gather | solution.py:33
  8.0 437.0 %all-gather.9.cloned.1.call-start = ((), (), s32[]{:S(2)}) async-start(), calls=%async_computation.1 | async-start | bytes 1597440 | tf_op jit(solution)/shard_map/all_gather | solution.py:34
  8.7 563.9 %all-gather.15.cloned.1.call-start = ((), (), s32[]{:S(2)}) async-start(), calls=%async_computation.4 | async-start | bytes 1597440 | tf_op jit(solution)/shard_map/all_gather | solution.py:57
  9.3 847.6 %all-reduce.2.cloned.1.call-start = ((), (), s32[]{:S(2)}) async-start(), calls=%async_computation | async-start | bytes 6291456 | tf_op jit(solution)/shard_map/psum | solution.py:47
Sparse Core Ops, SparseCore 0:
  10.3 144.8 all-gather.10
  158.1 136.2 all-gather.12
  297.3 136.2 all-gather.8
  436.5 136.1 all-gather.14
  576.0 280.9 all-reduce.1
where the time goes:
time: 876 us
  waiting for transfers between devices  683 us (78%)
  blocking collectives  142 us (16%)
  matrix products  16.4 us (2%)
  between operations  14.6 us (2%)
  local copies, waits for them, and re-layouts  13.7 us (2%)
    psum x1, waiting for transfers between devices, per_device(): summed, depth = lax.psum((partial_logits, count), 'depth')  282 us
    psum x1, blocking collectives, per_device(): summed, depth = lax.psum((partial_logits, count), 'depth')  142 us
    all_gather x1, waiting for transfers between devices, per_device(): lax.all_gather(probe_projector, 'depth', axis=0, tiled=True)  142 us
    all_gather x1, waiting for transfers between devices, per_device(): lax.all_gather(lookup_projector, 'depth', axis=0, tiled=True)  134 us
    all_gather x1, waiting for transfers between devices, per_device(): lax.all_gather(final_projector, 'depth', axis=0, tiled=True)  122 us
  transfers between devices with their start and end apart: 5, of which 4 were waited for; matrix products, arithmetic and copies ran while one was open for 3% of the time, Pallas kernels for 0%

commit v1 on v0

v1 whole, which is shorter than its diff:
```python
import functools
import math

import jax
import jax.numpy as jnp
from jax import lax
from jax.experimental import pallas as pl
from jax.experimental.pallas import tpu as pltpu
from jax.sharding import Mesh, PartitionSpec as P

D = 768
HEADS = 12
HD = 64
L = 256
NY, NC, NX, NZ = 4, 2, 4, 16
ND = NX * NZ
HX = HEADS // NX
WX = HX * HD
ROWS = D // ND
RY = ROWS // NY
BF = jnp.bfloat16
F32 = jnp.float32
VMEM = pl.BlockSpec(memory_space=pltpu.VMEM)
SMEM = pl.BlockSpec(memory_space=pltpu.SMEM)
VLIMIT = 24 * 1024 * 1024


def call(body, out, ins, scratch=(), flops=0, nbytes=1 << 20, name=None):
    return pl.pallas_call(
        body,
        out_shape=out,
        in_specs=ins,
        out_specs=jax.tree.map(lambda _: VMEM, out),
        scratch_shapes=list(scratch),
        compiler_params=pltpu.CompilerParams(vmem_limit_bytes=VLIMIT),
        cost_estimate=pl.CostEstimate(flops=flops, bytes_accessed=nbytes, transcendentals=0),
        name=name,
    )


def norm_body(tally, x_ref, scale_ref, out_ref):
    for r in range(2):
        x = x_ref[r * L : (r + 1) * L, :].astype(F32)
        mean = jnp.sum(x, axis=-1, keepdims=True) * (1.0 / D)
        x = x - mean
        var = jnp.sum(x * x, axis=-1, keepdims=True) * (1.0 / D)
        normed = (x * lax.rsqrt(var + 1e-05) * scale_ref[...]).astype(BF)
        live = (r < tally[0]).astype(BF)
        out_ref[r * L : (r + 1) * L, :] = normed * live


def pack_body(me, tally, q_ref, k_ref, v_ref, o_ref, out_ref, tile):
    y, first = me[1], me[2] == 0

    def rows(ref):
        all_rows = ref[...].astype(F32)
        got = all_rows[:RY]
        for i in range(1, NY):
            got = jnp.where(y == i, all_rows[i * RY : i * RY + RY], got)
        return got

    q, k, v, o = rows(q_ref), rows(k_ref), rows(v_ref), rows(o_ref)
    o = jnp.where(first, o[:, :384], o[:, 384:])
    count = jnp.full((1, 32), tally[0].astype(F32))
    for x in range(NX):
        mine = jnp.concatenate([w[:, WX * x : WX * x + WX] for w in (q, k, v)], axis=1)
        main = jnp.where(first, mine[:, :256], mine[:, 256:512])
        rest = jnp.where(first, mine[:, 512:544], mine[:, 544:576])
        for r in range(RY):
            for c in range(2):
                tile[2 * r + c : 2 * r + c + 1, :] = main[r : r + 1, 128 * c : 128 * c + 128]
            for c in range(3):
                tile[7 + 3 * r + c : 8 + 3 * r + c, :] = o[r : r + 1, 128 * c : 128 * c + 128]
        tile[6:7, :] = jnp.concatenate([rest[r : r + 1] for r in range(RY)] + [count], axis=1)
        made = tile[...].astype(BF)
        for z in range(NZ):
            out_ref[x * NZ + z] = made


def split_body(pieces_ref, early_ref, late_ref, count_ref):
    early = pieces_ref[:, 0:8, :]
    for y in range(NY):
        early_ref[y] = early
    late_ref[...] = pieces_ref[:, 8:16, :].reshape(ND * 8, 128)
    count_ref[...] = jnp.sum(early[:, 6, :].astype(F32), axis=0, keepdims=True)


def take(held, core, y, s):
    return held[core, y, pl.ds(s, ND, stride=8), :]


def in_body(me, own_ref, other_ref, w_ref, held, wide):
    core = me[2]
    held[core] = own_ref[...].astype(F32)
    held[1 - core] = other_ref[...].astype(F32)
    for y in range(NY):
        rest = [take(held, c, y, 6) for c in range(2)]
        for r in range(RY):
            rows = pl.ds(y * RY + r, ND, stride=ROWS)
            for k in range(4):
                wide[k, rows, :] = take(held, k // 2, y, 2 * r + k % 2)
            cut = [part[:, 32 * r : 32 * r + 32] for part in rest]
            wide[4, rows, :] = jnp.concatenate(cut + [jnp.zeros((ND, 64), F32)], axis=1)
    for k in range(5):
        w_ref[:, 128 * k : 128 * k + 128] = wide[k].astype(BF)


def out_body(me, own_a, other_a, own_b, other_b, w_ref, held_a, held_b, wide):
    y0, core = me[1], me[2]
    held_a[core] = own_a[...].astype(F32)
    held_a[1 - core] = other_a[...].astype(F32)
    for g, back in enumerate((0, 1, -1, 2)):
        y = (y0 - back + NY) % NY
        held_b[core, y] = own_b[g].astype(F32)
        held_b[1 - core, y] = other_b[g].astype(F32)
    for y in range(NY):
        for r in range(RY):
            rows = pl.ds(y * RY + r, ND, stride=ROWS)
            for c in range(2):
                for k in range(3):
                    s = 7 + 3 * r + k
                    wide[3 * c + k, rows, :] = take(held_a, c, y, s) if s < 8 else take(held_b, c, y, s - 8)
    for k in range(6):
        w_ref[:, 128 * k : 128 * k + 128] = wide[k].astype(BF)


def side_by_side(array, start):
    return jnp.concatenate([array[:L, start : start + HD], array[L:, start : start + HD]], axis=1)


def logits_body(x0, x1, x2, x3, x4, w_ref, s_ref, v_ref, total):
    project = lambda ref: jnp.dot(ref[...], w_ref[...], preferred_element_type=F32).astype(BF)
    for g in range(4):
        made = project((x0, x1, x2)[g]) if g < 3 else jnp.concatenate([project(x3), project(x4)], axis=0)
        for h in range(HX):
            q = side_by_side(made, h * HD)
            k = side_by_side(made, WX + h * HD)
            v_ref[h, :, 128 * g : 128 * g + 128] = side_by_side(made, 2 * WX + h * HD)
            s = lax.dot_general(q, k, (((1,), (1,)), ((), ())), preferred_element_type=F32)
            if g == 0:
                total[h] = s
            elif g < 3:
                total[h] += s
            else:
                s_ref[:, 16 * h : 16 * h + 16, :] = (total[h] + s).astype(BF).reshape(NZ, 16, L)


def softmax_body(count_ref, s_ref, p_ref):
    depth = count_ref[...][:, 96:97]
    s = s_ref[0].astype(F32)
    for z in range(1, NZ):
        s = s + s_ref[z].astype(F32)
    s = s / (math.sqrt(HD) * jnp.sqrt(depth))
    e = jnp.exp(s - jnp.max(s, axis=-1, keepdims=True))
    p = (e / jnp.sum(e, axis=-1, keepdims=True)).astype(BF)
    for z in range(NZ):
        p_ref[z] = p


def context_body(me, p_ref, v_ref, c_ref):
    x = me[0]
    for h in range(HX):
        p = p_ref[:, 16 * h : 16 * h + 16, :].reshape(L, L)
        made = jnp.dot(p, v_ref[h], preferred_element_type=F32).astype(BF)
        for g, back in enumerate((0, 1, -1, 2)):
            to = (x - back + NX) % NX
            c_ref[to, :, 128 * h : 128 * h + 128] = made[:, 128 * g : 128 * g + 128]


def mixed_body(tally, c_ref, w_ref, out_ref):
    chunks = [c_ref[h // HX, :, 128 * (h % HX) : 128 * (h % HX) + 128] for h in range(HEADS)]
    for r in range(2):
        a = jnp.concatenate([chunk[:, HD * r : HD * r + HD] for chunk in chunks], axis=1)
        made = jnp.dot(a, w_ref[...], preferred_element_type=F32)
        out_ref[r] = (made * (r < tally[0]).astype(F32)).astype(BF)


def struct(shape, dtype=BF):
    return jax.ShapeDtypeStruct(shape, dtype)


def per_device(x, scale, probe, lookup, content, final, tally):
    me = jnp.stack([lax.axis_index("x"), lax.axis_index("y"), lax.axis_index("core")]).astype(jnp.int32)
    shift = lambda a, axis, n, d: lax.ppermute(a, axis, [(i, (i + d) % n) for i in range(n)])
    fence = lambda *a: lax.optimization_barrier(a)

    pieces = call(pack_body, struct((ND, 16, 128)), [SMEM, SMEM] + [VMEM] * 4, [pltpu.VMEM((16, 128), F32)], name="pack")(
        me, tally, probe, lookup, content, final
    )
    normed = call(norm_body, struct((2 * L, D)), [SMEM, VMEM, VMEM], flops=1 << 22, nbytes=1 << 21, name="norm")(
        tally, x.reshape(2 * L, D), scale.reshape(1, D)
    )
    pieces = lax.all_to_all(pieces, ("x", "z"), 0, 0, tiled=True)
    near, far = shift(normed, "x", NX, 1), shift(normed, "x", NX, -1)
    over, under = shift(near[:L], "x", NX, 1), shift(far[L:], "x", NX, -1)

    pieces, over, under = fence(pieces, over, under)
    early, late, count = call(
        split_body,
        (struct((NY, ND, 8, 128)), struct((ND * 8, 128)), struct((1, 128), F32)),
        [VMEM],
        name="split",
    )(pieces)
    own = lax.all_to_all(early, "y", 0, 0, tiled=True)
    other = shift(own, "core", 2, 1)
    own, other = own.reshape(NY, ND * 8, 128), other.reshape(NY, ND * 8, 128)
    held = pltpu.VMEM((2, NY, ND * 8, 128), F32)
    wide = pltpu.VMEM((6, D, 128), F32)
    w_in = call(in_body, struct((D, 640)), [SMEM, VMEM, VMEM], [held, wide], 1 << 20, 1 << 22, name="unpack_in")(
        me, own, other
    )
    s, v = call(
        logits_body,
        (struct((NZ, 16 * HX, L)), struct((HX, L, 8 * HD))),
        [VMEM] * 6,
        [pltpu.VMEM((HX, L, L), F32)],
        flops=3 << 30,
        nbytes=1 << 23,
        name="logits",
    )(normed, near, far, over, under, w_in)

    s, late = fence(s, late)
    lates = [late] + [shift(late, "y", NY, d) for d in (1, -1, 2)]
    s = lax.all_to_all(s, "z", 0, 0, tiled=True)
    s, *lates = fence(s, *lates)
    p = call(softmax_body, struct((NZ, 16 * HX, L)), [VMEM, VMEM], flops=1 << 20, name="softmax")(count, s)
    own_late = jnp.stack(lates)
    p, own_late = fence(p, own_late)
    other_late = shift(own_late, "core", 2, 1)
    p = lax.all_to_all(p, "z", 0, 0, tiled=True)
    p, other_late = fence(p, other_late)
    c = call(context_body, struct((NX, L, 2 * WX)), [SMEM, VMEM, VMEM], flops=1 << 29, name="context")(me, p, v)
    w_out = call(out_body, struct((D, D)), [SMEM] + [VMEM] * 4, [held, held, wide], 1 << 20, 1 << 22, name="unpack_out")(
        me, own, other, own_late, other_late
    )
    c = lax.all_to_all(c, "x", 0, 0, tiled=True)
    return call(mixed_body, struct((2, L, D)), [SMEM, VMEM, VMEM], flops=1 << 30, name="mix")(tally, c, w_out)


def solution(mesh):
    axes = ("y", "core", "x", "z")
    grid = Mesh(mesh.devices.reshape(NY, NC, NX, NZ), axes)
    weight = P(("x", "z"), None)
    return jax.shard_map(
        per_device,
        mesh=grid,
        in_specs=(P(axes, None, None), P(), weight, weight, weight, weight, P(axes)),
        out_specs=P(axes, None, None),
        check_vma=False,
    )
```

time: 876 us -> 157 us (0.18)
  the two profiles are of different devices: /device:TPU:8 before, /device:TPU:32 now
where the time goes in v1:
time: 157 us
  starting transfers between devices  67.1 us (43%)
  waiting for transfers between devices  54.9 us (35%)
  Pallas kernels  13.5 us (9%)
  blocking collectives  12.3 us (8%)
  local copies, waits for them, and re-layouts  7.63 us (5%)
    ppermute x9, starting transfers between devices, per_device(): lax.ppermute(a, axis, [(i, (i + d) % n) for i in range(n)])  26.2 us
    all_to_all x1, starting transfers between devices, per_device(): pieces = lax.all_to_all(pieces, ('x', 'z'), 0, 0, tiled=True)  18.4 us
    all_to_all x1, waiting for transfers between devices, per_device(): p = lax.all_to_all(p, 'z', 0, 0, tiled=True)  17.6 us
    all_to_all x1, blocking collectives, per_device(): own = lax.all_to_all(early, 'y', 0, 0, tiled=True)  12.3 us
    all_to_all x1, waiting for transfers between devices, per_device(): pieces = lax.all_to_all(pieces, ('x', 'z'), 0, 0, tiled=True)  11.5 us
    all_to_all x1, starting transfers between devices, per_device(): s = lax.all_to_all(s, 'z', 0, 0, tiled=True)  11.1 us
    ppermute x9, waiting for transfers between devices, per_device(): lax.ppermute(a, axis, [(i, (i + d) % n) for i in range(n)])  9.9 us
    all_to_all x1, waiting for transfers between devices, per_device(): c = lax.all_to_all(c, 'x', 0, 0, tiled=True)  8.89 us
  transfers between devices with their start and end apart: 13, of which 8 were waited for; matrix products, arithmetic and copies ran while one was open for 1% of the time, Pallas kernels for 2%

profile of v1, /device:TPU:32, one launch (start us, length us, event | category | flops | bytes accessed | tf_op | source)
XLA Modules:
  0.0 156.5 jit_solution(5634245881374433140)
XLA Ops:
  3.1 4.7 %collective-permute-start.2 = (bf16[512,768]{1,0:T(8,128)(2,1)S(1)}, bf16[512,768]{1,0:T(8,128)(2,1)S(1)}, u32[]{:S(2)}, u32[]{:S(2)}) collective-permute-start(bf16[512,768]{1,0:T(8,128)(2,1)S(1)} %norm.1.x0), channel_id=1, source_target_pairs={{0,48},{16,0},{32,16},{48,32},{1,49},{17,1},{33,17},{49,33},{2,50}... | collective-permute-start | bytes 2359304 | tf_op jit(solution)/shard_map/ppermute | solution.py:184
  7.7 1.9 %collective-permute-start = (bf16[512,768]{1,0:T(8,128)(2,1)S(1)}, bf16[512,768]{1,0:T(8,128)(2,1)S(1)}, u32[]{:S(2)}, u32[]{:S(2)}) collective-permute-start(bf16[512,768]{1,0:T(8,128)(2,1)S(1)} %norm.1.x0), channel_id=1, source_target_pairs={{0,16},{16,32},{32,48},{48,0},{1,17},{17,33},{33,49},{49,1},{2,18}... | collective-permute-start | bytes 2359304 | tf_op jit(solution)/shard_map/ppermute | solution.py:184
  11.3 18.4 %all-to-all-start = ((bf16[64,16,128]{2,1,0:T(8,128)(2,1)}), bf16[64,16,128]{2,1,0:T(8,128)(2,1)S(1)}, u32[]{:S(2)}, u32[]{:S(2)}) async-start(bf16[64,16,128]{2,1,0:T(8,128)(2,1)} %pack.1), calls=%async_computation | async-start | bytes 524288 | tf_op jit(solution)/shard_map/all_to_all | solution.py:193
  30.5 4.8 %collective-permute-start.3 = (bf16[256,768]{1,0:T(8,128)(2,1)}, bf16[256,768]{1,0:T(8,128)(2,1)S(1)}, u32[]{:S(2)}, u32[]{:S(2)}) collective-permute-start(bf16[256,768]{1,0:T(8,128)(2,1)} %slice.9), channel_id=1, source_target_pairs={{0,48},{16,0},{32,16},{48,32},{1,49},{17,1},{33,17},{49,33},{2,50}... | collective-permute-start | bytes 1179656 | tf_op jit(solution)/shard_map/ppermute | solution.py:184
  36.1 1.9 %collective-permute-start.1 = (bf16[256,768]{1,0:T(8,128)(2,1)}, bf16[256,768]{1,0:T(8,128)(2,1)S(1)}, u32[]{:S(2)}, u32[]{:S(2)}) collective-permute-start(bf16[256,768]{1,0:T(8,128)(2,1)} %slice.8), channel_id=1, source_target_pairs={{0,16},{16,32},{32,48},{48,0},{1,17},{17,33},{33,49},{49,1},{2,18}... | collective-permute-start | bytes 1179656 | tf_op jit(solution)/shard_map/ppermute | solution.py:184
  38.0 11.5 %all-to-all-done.pieces_ref = bf16[64,16,128]{2,1,0:T(8,128)(2,1)S(1)} async-done(((bf16[64,16,128]{2,1,0:T(8,128)(2,1)}), bf16[64,16,128]{2,1,0:T(8,128)(2,1)S(1)}, u32[]{:S(2)}, u32[]{:S(2)}) %all-to-all-start) | async-done | bytes 262176 | tf_op jit(solution)/shard_map/all_to_all | solution.py:193
  51.1 12.3 %all_to_all.25 = bf16[4,64,8,128]{3,2,1,0:T(8,128)(2,1)S(1)} all-to-all(bf16[4,64,8,128]{3,2,1,0:T(8,128)(2,1)S(1)} %get-tuple-element.28), channel_id=1, replica_groups=mesh['y'=4,'core'=2,'x'=4,'z'=16] {'y'}, dimensions={0} | all-to-all | bytes 1048576 | tf_op jit(solution)/shard_map/all_to_all | solution.py:204
  63.4 2.0 %collective-permute-start.4 = (bf16[4,64,8,128]{3,2,1,0:T(8,128)(2,1)S(1)}, bf16[4,64,8,128]{3,2,1,0:T(8,128)(2,1)S(1)}, u32[]{:S(2)}, u32[]{:S(2)}) collective-permute-start(bf16[4,64,8,128]{3,2,1,0:T(8,128)(2,1)S(1)} %all_to_all.25), channel_id=1, source_target_pairs={{0,64},{64,0},{1,65},{65,1},{2,66},{66,2},{3,67},{67,3},{4,68},{68... | collective-permute-start | bytes 1572872 | tf_op jit(solution)/shard_map/ppermute | solution.py:184
  65.5 1.9 %collective-permute-done.4 = bf16[4,64,8,128]{3,2,1,0:T(8,128)(2,1)S(1)} collective-permute-done((bf16[4,64,8,128]{3,2,1,0:T(8,128)(2,1)S(1)}, bf16[4,64,8,128]{3,2,1,0:T(8,128)(2,1)S(1)}, u32[]{:S(2)}, u32[]{:S(2)}) %collective-permute-start.4) | collective-permute-done | bytes 524320 | tf_op jit(solution)/shard_map/ppermute | solution.py:184
  68.6 4.1 %logits.1 = (bf16[16,48,256]{2,1,0:T(8,128)(2,1)}, bf16[3,256,512]{2,1,0:T(8,128)(2,1)S(1)}) custom-call(bf16[512,768]{1,0:T(8,128)(2,1)S(1)} %norm.1.x0, bf16[512,768]{1,0:T(8,128)(2,1)S(1)} %collective-permute-done.x1, bf16[512,768]{1,0:T(8,128)(2,1)S(1)} %collective-permute-done.2.x2, bf16[256,768]{1,0:T(8,128)(2,1)S(1)} %copy-done.10, ...), custom_call_target="tpu_custom_call" | custom-call | flops 3221225472 | bytes 8388608 | tf_op jit(solution)/shard_map/logits/pallas_call | solution.py:212
  73.6 11.1 %all-to-all-start.2 = ((bf16[16,48,256]{2,1,0:T(8,128)(2,1)}), bf16[16,48,256]{2,1,0:T(8,128)(2,1)S(1)}, u32[]{:S(2)}, u32[]{:S(2)}) async-start(bf16[16,48,256]{2,1,0:T(8,128)(2,1)} %get-tuple-element.31), calls=%async_computation.2 | async-start | bytes 786432 | tf_op jit(solution)/shard_map/all_to_all | solution.py:224
  84.8 2.7 %collective-permute-start.7 = (bf16[512,128]{1,0:T(8,128)(2,1)S(1)}, bf16[512,128]{1,0:T(8,128)(2,1)S(1)}, u32[]{:S(2)}, u32[]{:S(2)}) collective-permute-start(bf16[512,128]{1,0:T(8,128)(2,1)S(1)} %get-tuple-element.34), channel_id=1, source_target_pairs={{0,256},{128,384},{256,0},{384,128},{1,257},{129,385},{257,1},{385... | collective-permute-start | bytes 393224 | tf_op jit(solution)/shard_map/ppermute | solution.py:184
  87.5 4.3 %collective-permute-start.6 = (bf16[512,128]{1,0:T(8,128)(2,1)S(1)}, bf16[512,128]{1,0:T(8,128)(2,1)S(1)}, u32[]{:S(2)}, u32[]{:S(2)}) collective-permute-start(bf16[512,128]{1,0:T(8,128)(2,1)S(1)} %get-tuple-element.34), channel_id=1, source_target_pairs={{0,384},{128,0},{256,128},{384,256},{1,385},{129,1},{257,129},{385... | collective-permute-start | bytes 393224 | tf_op jit(solution)/shard_map/ppermute | solution.py:184
  91.8 1.9 %collective-permute-start.5 = (bf16[512,128]{1,0:T(8,128)(2,1)S(1)}, bf16[512,128]{1,0:T(8,128)(2,1)S(1)}, u32[]{:S(2)}, u32[]{:S(2)}) collective-permute-start(bf16[512,128]{1,0:T(8,128)(2,1)S(1)} %get-tuple-element.34), channel_id=1, source_target_pairs={{0,128},{128,256},{256,384},{384,0},{1,129},{129,257},{257,385},{3... | collective-permute-start | bytes 393224 | tf_op jit(solution)/shard_map/ppermute | solution.py:184
  94.4 5.5 %collective-permute-done.5 = bf16[512,128]{1,0:T(8,128)(2,1)S(1)} collective-permute-done((bf16[512,128]{1,0:T(8,128)(2,1)S(1)}, bf16[512,128]{1,0:T(8,128)(2,1)S(1)}, u32[]{:S(2)}, u32[]{:S(2)}) %collective-permute-start.5) | collective-permute-done | bytes 131104 | tf_op jit(solution)/shard_map/ppermute | solution.py:184
  99.9 7.1 %all-to-all-done.2.s_ref = bf16[16,48,256]{2,1,0:T(8,128)(2,1)S(1)} async-done(((bf16[16,48,256]{2,1,0:T(8,128)(2,1)}), bf16[16,48,256]{2,1,0:T(8,128)(2,1)S(1)}, u32[]{:S(2)}, u32[]{:S(2)}) %all-to-all-start.2) | async-done | bytes 393248 | tf_op jit(solution)/shard_map/all_to_all | solution.py:224
  108.0 7.9 %all-to-all-start.3 = ((bf16[16,48,256]{2,1,0:T(8,128)(2,1)}), bf16[16,48,256]{2,1,0:T(8,128)(2,1)S(1)}, u32[]{:S(2)}, u32[]{:S(2)}) async-start(bf16[16,48,256]{2,1,0:T(8,128)(2,1)} %softmax.1), calls=%async_computation.3 | async-start | bytes 786432 | tf_op jit(solution)/shard_map/all_to_all | solution.py:230
  115.9 1.9 %collective-permute-start.8 = (bf16[4,512,128]{2,1,0:T(8,128)(2,1)S(1)}, bf16[4,512,128]{2,1,0:T(8,128)(2,1)S(1)}, u32[]{:S(2)}, u32[]{:S(2)}) collective-permute-start(bf16[4,512,128]{2,1,0:T(8,128)(2,1)S(1)} %pad_maximum_fusion.own_b), channel_id=1, source_target_pairs={{0,64},{64,0},{1,65},{65,1},{2,66},{66,2},{3,67},{67,3},{4,68},{68... | collective-permute-start | bytes 1572872 | tf_op jit(solution)/shard_map/ppermute | solution.py:184
  117.9 1.9 %collective-permute-done.8.other_b = bf16[4,512,128]{2,1,0:T(8,128)(2,1)S(1)} collective-permute-done((bf16[4,512,128]{2,1,0:T(8,128)(2,1)S(1)}, bf16[4,512,128]{2,1,0:T(8,128)(2,1)S(1)}, u32[]{:S(2)}, u32[]{:S(2)}) %collective-permute-start.8) | collective-permute-done | bytes 524320 | tf_op jit(solution)/shard_map/ppermute | solution.py:184
  120.5 17.6 %all-to-all-done.3.p_ref = bf16[16,48,256]{2,1,0:T(8,128)(2,1)S(1)} async-done(((bf16[16,48,256]{2,1,0:T(8,128)(2,1)}), bf16[16,48,256]{2,1,0:T(8,128)(2,1)S(1)}, u32[]{:S(2)}, u32[]{:S(2)}) %all-to-all-start.3) | async-done | bytes 393248 | tf_op jit(solution)/shard_map/all_to_all | solution.py:230
  138.1 1.8 %context.1 = bf16[4,256,384]{2,1,0:T(8,128)(2,1)} custom-call(s32[3]{0:T(128)S(1)} %pad_add_fusion.me, bf16[16,48,256]{2,1,0:T(8,128)(2,1)S(1)} %all-to-all-done.3.p_ref, bf16[3,256,512]{2,1,0:T(8,128)(2,1)S(1)} %copy-done.12), custom_call_target="tpu_custom_call" | custom-call | flops 536870912 | bytes 1048576 | tf_op jit(solution)/shard_map/context/pallas_call | solution.py:232
  140.0 3.5 %all-to-all-start.4 = ((bf16[4,256,384]{2,1,0:T(8,128)(2,1)}), bf16[4,256,384]{2,1,0:T(8,128)(2,1)S(1)}, u32[]{:S(2)}, u32[]{:S(2)}) async-start(bf16[4,256,384]{2,1,0:T(8,128)(2,1)} %context.1), calls=%async_computation.4 | async-start | bytes 1572864 | tf_op jit(solution)/shard_map/all_to_all | solution.py:236
  145.9 8.9 %all-to-all-done.4.c_ref = bf16[4,256,384]{2,1,0:T(8,128)(2,1)S(1)} async-done(((bf16[4,256,384]{2,1,0:T(8,128)(2,1)}), bf16[4,256,384]{2,1,0:T(8,128)(2,1)S(1)}, u32[]{:S(2)}, u32[]{:S(2)}) %all-to-all-start.4) | async-done | bytes 786464 | tf_op jit(solution)/shard_map/all_to_all | solution.py:236
  154.8 1.7 %mix.1 = bf16[2,256,768]{2,1,0:T(8,128)(2,1)} custom-call(s32[1]{0:T(128)S(6)} %copy.8.tally, bf16[4,256,384]{2,1,0:T(8,128)(2,1)S(1)} %all-to-all-done.4.c_ref, bf16[768,768]{1,0:T(8,128)(2,1)S(1)} %unpack_out.1.w_ref), custom_call_target="tpu_custom_call" | custom-call | flops 1073741824 | bytes 1048576 | tf_op jit(solution)/shard_map/mix/pallas_call | solution.py:237
  (43 shorter events, 14.3 us)
Async XLA Ops:
  1.3 1.1 copy-start
  2.5 7.3 %copy-start.3 = (bf16[12,768]{1,0:T(8,128)(2,1)S(1)}, bf16[12,768]{1,0:T(8,128)(2,1)}, u32[]{:S(2)}) copy-start(bf16[12,768]{1,0:T(8,128)(2,1)} %q_ref.1) | copy-start | bytes 55300
  2.5 7.3 %copy-start.4 = (bf16[12,768]{1,0:T(8,128)(2,1)S(1)}, bf16[12,768]{1,0:T(8,128)(2,1)}, u32[]{:S(2)}) copy-start(bf16[12,768]{1,0:T(8,128)(2,1)} %k_ref.1) | copy-start | bytes 55300
  2.5 7.3 %copy-start.5 = (bf16[12,768]{1,0:T(8,128)(2,1)S(1)}, bf16[12,768]{1,0:T(8,128)(2,1)}, u32[]{:S(2)}) copy-start(bf16[12,768]{1,0:T(8,128)(2,1)} %v_ref.1) | copy-start | bytes 55300
  2.5 7.3 %copy-start.6 = (bf16[12,768]{1,0:T(8,128)(2,1)S(1)}, bf16[12,768]{1,0:T(8,128)(2,1)}, u32[]{:S(2)}) copy-start(bf16[12,768]{1,0:T(8,128)(2,1)} %o_ref.1) | copy-start | bytes 55300
  3.1 26.6 %collective-permute-start.2 = (bf16[512,768]{1,0:T(8,128)(2,1)S(1)}, bf16[512,768]{1,0:T(8,128)(2,1)S(1)}, u32[]{:S(2)}, u32[]{:S(2)}) collective-permute-start(bf16[512,768]{1,0:T(8,128)(2,1)S(1)} %norm.1.x0), channel_id=1, source_target_pairs={{0,48},{16,0},{32,16},{48,32},{1,49},{17,1},{33,17},{49,33},{2,50}... | collective-permute-start | bytes 2359304 | tf_op jit(solution)/shard_map/ppermute | solution.py:184
  7.7 27.5 %collective-permute-start = (bf16[512,768]{1,0:T(8,128)(2,1)S(1)}, bf16[512,768]{1,0:T(8,128)(2,1)S(1)}, u32[]{:S(2)}, u32[]{:S(2)}) collective-permute-start(bf16[512,768]{1,0:T(8,128)(2,1)S(1)} %norm.1.x0), channel_id=1, source_target_pairs={{0,16},{16,32},{32,48},{48,0},{1,17},{17,33},{33,49},{49,1},{2,18}... | collective-permute-start | bytes 2359304 | tf_op jit(solution)/shard_map/ppermute | solution.py:184
  11.3 38.2 %all-to-all-start = ((bf16[64,16,128]{2,1,0:T(8,128)(2,1)}), bf16[64,16,128]{2,1,0:T(8,128)(2,1)S(1)}, u32[]{:S(2)}, u32[]{:S(2)}) async-start(bf16[64,16,128]{2,1,0:T(8,128)(2,1)} %pack.1), calls=%async_computation | async-start | bytes 524288 | tf_op jit(solution)/shard_map/all_to_all | solution.py:193
  30.5 19.0 %collective-permute-start.3 = (bf16[256,768]{1,0:T(8,128)(2,1)}, bf16[256,768]{1,0:T(8,128)(2,1)S(1)}, u32[]{:S(2)}, u32[]{:S(2)}) collective-permute-start(bf16[256,768]{1,0:T(8,128)(2,1)} %slice.9), channel_id=1, source_target_pairs={{0,48},{16,0},{32,16},{48,32},{1,49},{17,1},{33,17},{49,33},{2,50}... | collective-permute-start | bytes 1179656 | tf_op jit(solution)/shard_map/ppermute | solution.py:184
  36.1 14.2 %collective-permute-start.1 = (bf16[256,768]{1,0:T(8,128)(2,1)}, bf16[256,768]{1,0:T(8,128)(2,1)S(1)}, u32[]{:S(2)}, u32[]{:S(2)}) collective-permute-start(bf16[256,768]{1,0:T(8,128)(2,1)} %slice.8), channel_id=1, source_target_pairs={{0,16},{16,32},{32,48},{48,0},{1,17},{17,33},{33,49},{49,1},{2,18}... | collective-permute-start | bytes 1179656 | tf_op jit(solution)/shard_map/ppermute | solution.py:184
  63.4 5.2 %copy-start.8 = (bf16[256,768]{1,0:T(8,128)(2,1)S(1)}, bf16[256,768]{1,0:T(8,128)(2,1)}, u32[]{:S(2)}) copy-start(bf16[256,768]{1,0:T(8,128)(2,1)} %copy-done.7) | copy-start | bytes 1179652
  63.4 5.2 %copy-start.10 = (bf16[256,768]{1,0:T(8,128)(2,1)S(1)}, bf16[256,768]{1,0:T(8,128)(2,1)}, u32[]{:S(2)}) copy-start(bf16[256,768]{1,0:T(8,128)(2,1)} %copy-done.9) | copy-start | bytes 1179652
  63.4 3.9 %collective-permute-start.4 = (bf16[4,64,8,128]{3,2,1,0:T(8,128)(2,1)S(1)}, bf16[4,64,8,128]{3,2,1,0:T(8,128)(2,1)S(1)}, u32[]{:S(2)}, u32[]{:S(2)}) collective-permute-start(bf16[4,64,8,128]{3,2,1,0:T(8,128)(2,1)S(1)} %all_to_all.25), channel_id=1, source_target_pairs={{0,64},{64,0},{1,65},{65,1},{2,66},{66,2},{3,67},{67,3},{4,68},{68... | collective-permute-start | bytes 1572872 | tf_op jit(solution)/shard_map/ppermute | solution.py:184
  72.7 0.9 copy-start.11
  73.6 33.3 %all-to-all-start.2 = ((bf16[16,48,256]{2,1,0:T(8,128)(2,1)}), bf16[16,48,256]{2,1,0:T(8,128)(2,1)S(1)}, u32[]{:S(2)}, u32[]{:S(2)}) async-start(bf16[16,48,256]{2,1,0:T(8,128)(2,1)} %get-tuple-element.31), calls=%async_computation.2 | async-start | bytes 786432 | tf_op jit(solution)/shard_map/all_to_all | solution.py:224
  84.8 9.0 %collective-permute-start.7 = (bf16[512,128]{1,0:T(8,128)(2,1)S(1)}, bf16[512,128]{1,0:T(8,128)(2,1)S(1)}, u32[]{:S(2)}, u32[]{:S(2)}) collective-permute-start(bf16[512,128]{1,0:T(8,128)(2,1)S(1)} %get-tuple-element.34), channel_id=1, source_target_pairs={{0,256},{128,384},{256,0},{384,128},{1,257},{129,385},{257,1},{385... | collective-permute-start | bytes 393224 | tf_op jit(solution)/shard_map/ppermute | solution.py:184
  87.5 6.9 %collective-permute-start.6 = (bf16[512,128]{1,0:T(8,128)(2,1)S(1)}, bf16[512,128]{1,0:T(8,128)(2,1)S(1)}, u32[]{:S(2)}, u32[]{:S(2)}) collective-permute-start(bf16[512,128]{1,0:T(8,128)(2,1)S(1)} %get-tuple-element.34), channel_id=1, source_target_pairs={{0,384},{128,0},{256,128},{384,256},{1,385},{129,1},{257,129},{385... | collective-permute-start | bytes 393224 | tf_op jit(solution)/shard_map/ppermute | solution.py:184
  91.8 8.1 %collective-permute-start.5 = (bf16[512,128]{1,0:T(8,128)(2,1)S(1)}, bf16[512,128]{1,0:T(8,128)(2,1)S(1)}, u32[]{:S(2)}, u32[]{:S(2)}) collective-permute-start(bf16[512,128]{1,0:T(8,128)(2,1)S(1)} %get-tuple-element.34), channel_id=1, source_target_pairs={{0,128},{128,256},{256,384},{384,0},{1,129},{129,257},{257,385},{3... | collective-permute-start | bytes 393224 | tf_op jit(solution)/shard_map/ppermute | solution.py:184
  106.9 31.2 %copy-start.12 = (bf16[3,256,512]{2,1,0:T(8,128)(2,1)S(1)}, bf16[3,256,512]{2,1,0:T(8,128)(2,1)}, u32[]{:S(2)}) copy-start(bf16[3,256,512]{2,1,0:T(8,128)(2,1)} %copy-done.11) | copy-start | bytes 2359300
  108.0 30.1 %all-to-all-start.3 = ((bf16[16,48,256]{2,1,0:T(8,128)(2,1)}), bf16[16,48,256]{2,1,0:T(8,128)(2,1)S(1)}, u32[]{:S(2)}, u32[]{:S(2)}) async-start(bf16[16,48,256]{2,1,0:T(8,128)(2,1)} %softmax.1), calls=%async_computation.3 | async-start | bytes 786432 | tf_op jit(solution)/shard_map/all_to_all | solution.py:230
  115.9 3.8 %collective-permute-start.8 = (bf16[4,512,128]{2,1,0:T(8,128)(2,1)S(1)}, bf16[4,512,128]{2,1,0:T(8,128)(2,1)S(1)}, u32[]{:S(2)}, u32[]{:S(2)}) collective-permute-start(bf16[4,512,128]{2,1,0:T(8,128)(2,1)S(1)} %pad_maximum_fusion.own_b), channel_id=1, source_target_pairs={{0,64},{64,0},{1,65},{65,1},{2,66},{66,2},{3,67},{67,3},{4,68},{68... | collective-permute-start | bytes 1572872 | tf_op jit(solution)/shard_map/ppermute | solution.py:184
  119.7 0.8 copy-start.1
  140.0 14.9 %all-to-all-start.4 = ((bf16[4,256,384]{2,1,0:T(8,128)(2,1)}), bf16[4,256,384]{2,1,0:T(8,128)(2,1)S(1)}, u32[]{:S(2)}, u32[]{:S(2)}) async-start(bf16[4,256,384]{2,1,0:T(8,128)(2,1)} %context.1), calls=%async_computation.4 | async-start | bytes 1572864 | tf_op jit(solution)/shard_map/all_to_all | solution.py:236
  143.5 1.0 copy-start.2
  (2 other events, 1.5 us)

commit v2 on v1

--- a/solution.py
+++ b/solution.py
@@ -21,45 +21,43 @@
 BF = jnp.bfloat16
 F32 = jnp.float32
 VMEM = pl.BlockSpec(memory_space=pltpu.VMEM)
+ANY = pl.BlockSpec()
+HBM = pl.BlockSpec(memory_space=pltpu.HBM)
 SMEM = pl.BlockSpec(memory_space=pltpu.SMEM)
 VLIMIT = 24 * 1024 * 1024
-
-
-def call(body, out, ins, scratch=(), flops=0, nbytes=1 << 20, name=None):
+VMOST = 60 * 1024 * 1024
+
+
+def call(body, out, ins, scratch=(), flops=0, nbytes=1 << 20, name=None, outs=None, limit=VLIMIT):
     return pl.pallas_call(
         body,
         out_shape=out,
         in_specs=ins,
-        out_specs=jax.tree.map(lambda _: VMEM, out),
+        out_specs=outs or jax.tree.map(lambda _: VMEM, out),
         scratch_shapes=list(scratch),
-        compiler_params=pltpu.CompilerParams(vmem_limit_bytes=VLIMIT),
+        compiler_params=pltpu.CompilerParams(vmem_limit_bytes=limit),
         cost_estimate=pl.CostEstimate(flops=flops, bytes_accessed=nbytes, transcendentals=0),
         name=name,
     )
 
 
-def norm_body(tally, x_ref, scale_ref, out_ref):
-    for r in range(2):
-        x = x_ref[r * L : (r + 1) * L, :].astype(F32)
-        mean = jnp.sum(x, axis=-1, keepdims=True) * (1.0 / D)
-        x = x - mean
-        var = jnp.sum(x * x, axis=-1, keepdims=True) * (1.0 / D)
-        normed = (x * lax.rsqrt(var + 1e-05) * scale_ref[...]).astype(BF)
-        live = (r < tally[0]).astype(BF)
-        out_ref[r * L : (r + 1) * L, :] = normed * live
-
-
-def pack_body(me, tally, q_ref, k_ref, v_ref, o_ref, out_ref, tile):
-    y, first = me[1], me[2] == 0
-
-    def rows(ref):
-        all_rows = ref[...].astype(F32)
+def first_body(me, tally, x_hbm, g_hbm, q_hbm, k_hbm, v_hbm, o_hbm, out_ref, normed_ref, x_ref, g_ref, near, tile, sems):
+    y, first = me[0] // 128, me[0] // 64 % 2 == 0
+    weights = [pltpu.make_async_copy(w, near.at[i], sems.at[i]) for i, w in enumerate((q_hbm, k_hbm, v_hbm, o_hbm))]
+    others = [pltpu.make_async_copy(x_hbm, x_ref, sems.at[4]), pltpu.make_async_copy(g_hbm, g_ref, sems.at[5])]
+    for copy in weights + others:
+        copy.start()
+    for copy in weights:
+        copy.wait()
+
+    def rows(i):
+        all_rows = near[i].astype(F32)
         got = all_rows[:RY]
-        for i in range(1, NY):
-            got = jnp.where(y == i, all_rows[i * RY : i * RY + RY], got)
+        for j in range(1, NY):
+            got = jnp.where(y == j, all_rows[j * RY : j * RY + RY], got)
         return got
 
-    q, k, v, o = rows(q_ref), rows(k_ref), rows(v_ref), rows(o_ref)
+    q, k, v, o = (rows(i) for i in range(4))
     o = jnp.where(first, o[:, :384], o[:, 384:])
     count = jnp.full((1, 32), tally[0].astype(F32))
     for x in range(NX):
@@ -75,6 +73,17 @@
         made = tile[...].astype(BF)
         for z in range(NZ):
             out_ref[x * NZ + z] = made
+    for copy in others:
+        copy.wait()
+    scale = g_ref[...].reshape(1, D)
+    for r in range(2):
+        x = x_ref[r * L : (r + 1) * L, :].astype(F32)
+        mean = jnp.sum(x, axis=-1, keepdims=True) * (1.0 / D)
+        x = x - mean
+        var = jnp.sum(x * x, axis=-1, keepdims=True) * (1.0 / D)
+        normed = (x * lax.rsqrt(var + 1e-05) * scale).astype(BF)
+        live = (r < tally[0]).astype(BF)
+        normed_ref[r * L : (r + 1) * L, :] = normed * live
 
 
 def split_body(pieces_ref, early_ref, late_ref, count_ref):
@@ -90,7 +99,7 @@
 
 
 def in_body(me, own_ref, other_ref, w_ref, held, wide):
-    core = me[2]
+    core = me[0] // 64 % 2
     held[core] = own_ref[...].astype(F32)
     held[1 - core] = other_ref[...].astype(F32)
     for y in range(NY):
@@ -106,7 +115,7 @@
 
 
 def out_body(me, own_a, other_a, own_b, other_b, w_ref, held_a, held_b, wide):
-    y0, core = me[1], me[2]
+    y0, core = me[0] // 128, me[0] // 64 % 2
     held_a[core] = own_a[...].astype(F32)
     held_a[1 - core] = other_a[...].astype(F32)
     for g, back in enumerate((0, 1, -1, 2)):
@@ -128,10 +137,9 @@
     return jnp.concatenate([array[:L, start : start + HD], array[L:, start : start + HD]], axis=1)
 
 
-def logits_body(x0, x1, x2, x3, x4, w_ref, s_ref, v_ref, total):
-    project = lambda ref: jnp.dot(ref[...], w_ref[...], preferred_element_type=F32).astype(BF)
-    for g in range(4):
-        made = project((x0, x1, x2)[g]) if g < 3 else jnp.concatenate([project(x3), project(x4)], axis=0)
+def logits_body(x0, x1, x2, x3, w_ref, s_ref, v_ref, total):
+    for g, x_ref in enumerate((x0, x1, x2, x3)):
+        made = jnp.dot(x_ref[...], w_ref[...], preferred_element_type=F32).astype(BF)
         for h in range(HX):
             q = side_by_side(made, h * HD)
             k = side_by_side(made, WX + h * HD)
@@ -158,7 +166,7 @@
 
 
 def context_body(me, p_ref, v_ref, c_ref):
-    x = me[0]
+    x = me[0] // 16 % 4
     for h in range(HX):
         p = p_ref[:, 16 * h : 16 * h + 16, :].reshape(L, L)
         made = jnp.dot(p, v_ref[h], preferred_element_type=F32).astype(BF)
@@ -180,21 +188,29 @@
 
 
 def per_device(x, scale, probe, lookup, content, final, tally):
-    me = jnp.stack([lax.axis_index("x"), lax.axis_index("y"), lax.axis_index("core")]).astype(jnp.int32)
+    me = lax.axis_index(("y", "core", "x", "z")).astype(jnp.int32).reshape(1)
     shift = lambda a, axis, n, d: lax.ppermute(a, axis, [(i, (i + d) % n) for i in range(n)])
     fence = lambda *a: lax.optimization_barrier(a)
 
-    pieces = call(pack_body, struct((ND, 16, 128)), [SMEM, SMEM] + [VMEM] * 4, [pltpu.VMEM((16, 128), F32)], name="pack")(
-        me, tally, probe, lookup, content, final
-    )
-    normed = call(norm_body, struct((2 * L, D)), [SMEM, VMEM, VMEM], flops=1 << 22, nbytes=1 << 21, name="norm")(
-        tally, x.reshape(2 * L, D), scale.reshape(1, D)
-    )
+    pieces, normed = call(
+        first_body,
+        (struct((ND, 16, 128)), struct((2 * L, D))),
+        [SMEM, SMEM] + [HBM] * 6,
+        [
+            pltpu.VMEM((2 * L, D), BF),
+            pltpu.VMEM((D,), F32),
+            pltpu.VMEM((4, ROWS, D), BF),
+            pltpu.VMEM((16, 128), F32),
+            pltpu.SemaphoreType.DMA((6,)),
+        ],
+        name="first",
+        outs=(ANY, ANY),
+        limit=VMOST,
+    )(me, tally, x.reshape(2 * L, D), scale, probe, lookup, content, final)
     pieces = lax.all_to_all(pieces, ("x", "z"), 0, 0, tiled=True)
     near, far = shift(normed, "x", NX, 1), shift(normed, "x", NX, -1)
-    over, under = shift(near[:L], "x", NX, 1), shift(far[L:], "x", NX, -1)
-
-    pieces, over, under = fence(pieces, over, under)
+    across = shift(near, "x", NX, 1)
+
     early, late, count = call(
         split_body,
         (struct((NY, ND, 8, 128)), struct((ND * 8, 128)), struct((1, 128), F32)),
@@ -202,6 +218,7 @@
         name="split",
     )(pieces)
     own = lax.all_to_all(early, "y", 0, 0, tiled=True)
+    own, far, across = fence(own, far, across)
     other = shift(own, "core", 2, 1)
     own, other = own.reshape(NY, ND * 8, 128), other.reshape(NY, ND * 8, 128)
     held = pltpu.VMEM((2, NY, ND * 8, 128), F32)
@@ -212,12 +229,12 @@
     s, v = call(
         logits_body,
         (struct((NZ, 16 * HX, L)), struct((HX, L, 8 * HD))),
-        [VMEM] * 6,
+        [VMEM] * 5,
         [pltpu.VMEM((HX, L, L), F32)],
         flops=3 << 30,
         nbytes=1 << 23,
         name="logits",
-    )(normed, near, far, over, under, w_in)
+    )(normed, near, far, across, w_in)
 
     s, late = fence(s, late)
     lates = [late] + [shift(late, "y", NY, d) for d in (1, -1, 2)]
@@ -228,11 +245,11 @@
     p, own_late = fence(p, own_late)
     other_late = shift(own_late, "core", 2, 1)
     p = lax.all_to_all(p, "z", 0, 0, tiled=True)
-    p, other_late = fence(p, other_late)
-    c = call(context_body, struct((NX, L, 2 * WX)), [SMEM, VMEM, VMEM], flops=1 << 29, name="context")(me, p, v)
     w_out = call(out_body, struct((D, D)), [SMEM] + [VMEM] * 4, [held, held, wide], 1 << 20, 1 << 22, name="unpack_out")(
         me, own, other, own_late, other_late
     )
+    p, w_out = fence(p, w_out)
+    c = call(context_body, struct((NX, L, 2 * WX)), [SMEM, VMEM, ANY], flops=1 << 29, name="context")(me, p, v)
     c = lax.all_to_all(c, "x", 0, 0, tiled=True)
     return call(mixed_body, struct((2, L, D)), [SMEM, VMEM, VMEM], flops=1 << 30, name="mix")(tally, c, w_out)
 

time: 157 us -> 146 us (0.930)
  starting transfers between devices: 67.1 us -> 60.3 us
  local copies, waits for them, and re-layouts: 7.63 us -> 2.94 us
  blocking collectives: 12.3 us -> 14.2 us
    all_to_all x1, starting transfers between devices: 11.1 us -> 5.5 us  [per_device(): s = lax.all_to_all(s, 'z', 0, 0, tiled=True)]
    unnamed x26 -> x10, local copies, waits for them, and re-layouts: 5.38 us -> 2.94 us
    all_to_all x1, blocking collectives: 12.3 us -> 14.2 us  [per_device(): c = lax.all_to_all(c, 'x', 0, 0, tiled=True)]
    all_to_all x1, waiting for transfers between devices: 11.5 us -> 13.3 us  [per_device(): pieces = lax.all_to_all(pieces, ('x', 'z'), 0, 0, tiled=True)]
    ppermute x9 -> x8, starting transfers between devices: 26.2 us -> 24.7 us  [per_device(): lax.ppermute(a, axis, [(i, (i + d) % n) for i in range(n)])]
    ppermute x9 -> x8, waiting for transfers between devices: 9.9 us -> 8.94 us  [per_device(): lax.ppermute(a, axis, [(i, (i + d) % n) for i in range(n)])]
    pallas_call x3 -> x2, Pallas kernels: 3.9 us -> 3.07 us  [the longest x1 2.66 us: per_device(): call(first_body, (struct((ND, 16, 128)), struct((2 * L, D))), [SMEM, SMEM...]
  transfers between devices with their start and end apart: 13 -> 12, of which waited for: 8 -> 8; matrix products, arithmetic and copies ran while one was open for 1% -> 0% of each run, Pallas kernels for 2% -> 1%
where the time goes in v2:
time: 146 us
  starting transfers between devices  60.3 us (41%)
  waiting for transfers between devices  53.8 us (37%)
  blocking collectives  14.2 us (10%)
  Pallas kernels  13.6 us (9%)
  local copies, waits for them, and re-layouts  2.94 us (2%)
    ppermute x8, starting transfers between devices, per_device(): lax.ppermute(a, axis, [(i, (i + d) % n) for i in range(n)])  24.7 us
    all_to_all x1, starting transfers between devices, per_device(): pieces = lax.all_to_all(pieces, ('x', 'z'), 0, 0, tiled=True)  17.9 us
    all_to_all x1, waiting for transfers between devices, per_device(): p = lax.all_to_all(p, 'z', 0, 0, tiled=True)  17.5 us
    all_to_all x1, blocking collectives, per_device(): c = lax.all_to_all(c, 'x', 0, 0, tiled=True)  14.2 us
    all_to_all x1, waiting for transfers between devices, per_device(): pieces = lax.all_to_all(pieces, ('x', 'z'), 0, 0, tiled=True)  13.3 us
    ppermute x8, waiting for transfers between devices, per_device(): lax.ppermute(a, axis, [(i, (i + d) % n) for i in range(n)])  8.94 us
    all_to_all x1, starting transfers between devices, per_device(): p = lax.all_to_all(p, 'z', 0, 0, tiled=True)  7.71 us
    all_to_all x1, waiting for transfers between devices, per_device(): own = lax.all_to_all(early, 'y', 0, 0, tiled=True)  7.5 us
  transfers between devices with their start and end apart: 12, of which 8 were waited for; matrix products, arithmetic and copies ran while one was open for 0% of the time, Pallas kernels for 1%

profile of v2, /device:TPU:32, one launch (start us, length us, event | category | flops | bytes accessed | tf_op | source)
XLA Modules:
  0.0 145.7 jit_solution(17883810685956855446)
XLA Ops:
  0.7 2.7 %first.1 = (bf16[64,16,128]{2,1,0:T(8,128)(2,1)}, bf16[512,768]{1,0:T(8,128)(2,1)}) custom-call(s32[1]{0:T(128)} %bitcast.me, s32[1]{0:T(128)S(6)} %copy.8.tally, bf16[512,768]{1,0:T(8,128)(2,1)} %bitcast.13, f32[768]{0:T(1024)} %g_hbm.1, bf16[12,768]{1,0:T(8,128)(2,1)} %q_hbm.1, bf16[12,768]{1,0:T(8,128)(2,1)} %k_hbm.1, bf16[12,768]{1,0:T(8,128)(2,1)} %v_hbm.1, ...), custom_call_target="tpu_custom_call" | custom-call | bytes 1048576 | tf_op jit(solution)/shard_map/first/pallas_call | solution.py:195
  3.3 3.4 %collective-permute-start = (bf16[512,768]{1,0:T(8,128)(2,1)}, bf16[512,768]{1,0:T(8,128)(2,1)S(1)}, u32[]{:S(2)}, u32[]{:S(2)}) collective-permute-start(bf16[512,768]{1,0:T(8,128)(2,1)} %get-tuple-element.28.x0), channel_id=1, source_target_pairs={{0,16},{16,32},{32,48},{48,0},{1,17},{17,33},{33,49},{49,1},{2,18}... | collective-permute-start | bytes 2359304 | tf_op jit(solution)/shard_map/ppermute | solution.py:192
  6.7 17.9 %all-to-all-start = ((bf16[64,16,128]{2,1,0:T(8,128)(2,1)}), bf16[64,16,128]{2,1,0:T(8,128)(2,1)S(1)}, u32[]{:S(2)}, u32[]{:S(2)}) async-start(bf16[64,16,128]{2,1,0:T(8,128)(2,1)} %get-tuple-element.26), calls=%async_computation | async-start | bytes 524288 | tf_op jit(solution)/shard_map/all_to_all | solution.py:210
  24.7 4.8 %collective-permute-start.1 = (bf16[512,768]{1,0:T(8,128)(2,1)}, bf16[512,768]{1,0:T(8,128)(2,1)S(1)}, u32[]{:S(2)}, u32[]{:S(2)}) collective-permute-start(bf16[512,768]{1,0:T(8,128)(2,1)} %get-tuple-element.28.x0), channel_id=1, source_target_pairs={{0,48},{16,0},{32,16},{48,32},{1,49},{17,1},{33,17},{49,33},{2,50}... | collective-permute-start | bytes 2359304 | tf_op jit(solution)/shard_map/ppermute | solution.py:192
  29.5 1.9 %collective-permute-start.2 = (bf16[512,768]{1,0:T(8,128)(2,1)S(1)}, bf16[512,768]{1,0:T(8,128)(2,1)}, u32[]{:S(2)}, u32[]{:S(2)}) collective-permute-start(bf16[512,768]{1,0:T(8,128)(2,1)S(1)} %collective-permute-done.x1), channel_id=1, source_target_pairs={{0,16},{16,32},{32,48},{48,0},{1,17},{17,33},{33,49},{49,1},{2,18}... | collective-permute-start | bytes 2359304 | tf_op jit(solution)/shard_map/ppermute | solution.py:192
  31.4 13.3 %all-to-all-done.pieces_ref = bf16[64,16,128]{2,1,0:T(8,128)(2,1)S(1)} async-done(((bf16[64,16,128]{2,1,0:T(8,128)(2,1)}), bf16[64,16,128]{2,1,0:T(8,128)(2,1)S(1)}, u32[]{:S(2)}, u32[]{:S(2)}) %all-to-all-start) | async-done | bytes 262176 | tf_op jit(solution)/shard_map/all_to_all | solution.py:210
  45.6 4.5 %all-to-all-start.1 = ((bf16[4,64,8,128]{3,2,1,0:T(8,128)(2,1)}), bf16[4,64,8,128]{3,2,1,0:T(8,128)(2,1)S(1)}, u32[]{:S(2)}, u32[]{:S(2)}) async-start(bf16[4,64,8,128]{3,2,1,0:T(8,128)(2,1)} %get-tuple-element.29), calls=%async_computation.1 | async-start | bytes 1048576 | tf_op jit(solution)/shard_map/all_to_all | solution.py:220
  51.0 7.5 %all-to-all-done.1 = bf16[4,64,8,128]{3,2,1,0:T(8,128)(2,1)S(1)} async-done(((bf16[4,64,8,128]{3,2,1,0:T(8,128)(2,1)}), bf16[4,64,8,128]{3,2,1,0:T(8,128)(2,1)S(1)}, u32[]{:S(2)}, u32[]{:S(2)}) %all-to-all-start.1) | async-done | bytes 524320 | tf_op jit(solution)/shard_map/all_to_all | solution.py:220
  58.5 2.0 %collective-permute-start.3 = (bf16[4,64,8,128]{3,2,1,0:T(8,128)(2,1)S(1)}, bf16[4,64,8,128]{3,2,1,0:T(8,128)(2,1)S(1)}, u32[]{:S(2)}, u32[]{:S(2)}) collective-permute-start(bf16[4,64,8,128]{3,2,1,0:T(8,128)(2,1)S(1)} %all-to-all-done.1), channel_id=1, source_target_pairs={{0,64},{64,0},{1,65},{65,1},{2,66},{66,2},{3,67},{67,3},{4,68},{68... | collective-permute-start | bytes 1572872 | tf_op jit(solution)/shard_map/ppermute | solution.py:192
  60.6 1.9 %collective-permute-done.3 = bf16[4,64,8,128]{3,2,1,0:T(8,128)(2,1)S(1)} collective-permute-done((bf16[4,64,8,128]{3,2,1,0:T(8,128)(2,1)S(1)}, bf16[4,64,8,128]{3,2,1,0:T(8,128)(2,1)S(1)}, u32[]{:S(2)}, u32[]{:S(2)}) %collective-permute-start.3) | collective-permute-done | bytes 524320 | tf_op jit(solution)/shard_map/ppermute | solution.py:192
  63.3 5.2 %logits.1 = (bf16[16,48,256]{2,1,0:T(8,128)(2,1)}, bf16[3,256,512]{2,1,0:T(8,128)(2,1)S(1)}) custom-call(bf16[512,768]{1,0:T(8,128)(2,1)S(1)} %copy-done, bf16[512,768]{1,0:T(8,128)(2,1)S(1)} %collective-permute-done.x1, bf16[512,768]{1,0:T(8,128)(2,1)S(1)} %copy-done.2, bf16[512,768]{1,0:T(8,128)(2,1)} %collective-permute-done.2.x3, ...), custom_call_target="tpu_custom_call" | custom-call | flops 3221225472 | bytes 8388608 | tf_op jit(solution)/shard_map/logits/pallas_call | solution.py:229
  69.4 5.5 %all-to-all-start.2 = ((bf16[16,48,256]{2,1,0:T(8,128)(2,1)}), bf16[16,48,256]{2,1,0:T(8,128)(2,1)S(1)}, u32[]{:S(2)}, u32[]{:S(2)}) async-start(bf16[16,48,256]{2,1,0:T(8,128)(2,1)} %get-tuple-element.35), calls=%async_computation.2 | async-start | bytes 786432 | tf_op jit(solution)/shard_map/all_to_all | solution.py:241
  74.8 4.8 %collective-permute-start.6 = (bf16[512,128]{1,0:T(8,128)(2,1)S(1)}, bf16[512,128]{1,0:T(8,128)(2,1)S(1)}, u32[]{:S(2)}, u32[]{:S(2)}) collective-permute-start(bf16[512,128]{1,0:T(8,128)(2,1)S(1)} %get-tuple-element.38), channel_id=1, source_target_pairs={{0,256},{128,384},{256,0},{384,128},{1,257},{129,385},{257,1},{385... | collective-permute-start | bytes 393224 | tf_op jit(solution)/shard_map/ppermute | solution.py:192
  79.6 3.0 %collective-permute-start.5 = (bf16[512,128]{1,0:T(8,128)(2,1)S(1)}, bf16[512,128]{1,0:T(8,128)(2,1)S(1)}, u32[]{:S(2)}, u32[]{:S(2)}) collective-permute-start(bf16[512,128]{1,0:T(8,128)(2,1)S(1)} %get-tuple-element.38), channel_id=1, source_target_pairs={{0,384},{128,0},{256,128},{384,256},{1,385},{129,1},{257,129},{385... | collective-permute-start | bytes 393224 | tf_op jit(solution)/shard_map/ppermute | solution.py:192
  82.6 2.9 %collective-permute-start.4 = (bf16[512,128]{1,0:T(8,128)(2,1)S(1)}, bf16[512,128]{1,0:T(8,128)(2,1)S(1)}, u32[]{:S(2)}, u32[]{:S(2)}) collective-permute-start(bf16[512,128]{1,0:T(8,128)(2,1)S(1)} %get-tuple-element.38), channel_id=1, source_target_pairs={{0,128},{128,256},{256,384},{384,0},{1,129},{129,257},{257,385},{3... | collective-permute-start | bytes 393224 | tf_op jit(solution)/shard_map/ppermute | solution.py:192
  86.5 4.2 %collective-permute-done.4 = bf16[512,128]{1,0:T(8,128)(2,1)S(1)} collective-permute-done((bf16[512,128]{1,0:T(8,128)(2,1)S(1)}, bf16[512,128]{1,0:T(8,128)(2,1)S(1)}, u32[]{:S(2)}, u32[]{:S(2)}) %collective-permute-start.4) | collective-permute-done | bytes 131104 | tf_op jit(solution)/shard_map/ppermute | solution.py:192
  90.7 6.5 %all-to-all-done.2.s_ref = bf16[16,48,256]{2,1,0:T(8,128)(2,1)S(1)} async-done(((bf16[16,48,256]{2,1,0:T(8,128)(2,1)}), bf16[16,48,256]{2,1,0:T(8,128)(2,1)S(1)}, u32[]{:S(2)}, u32[]{:S(2)}) %all-to-all-start.2) | async-done | bytes 393248 | tf_op jit(solution)/shard_map/all_to_all | solution.py:241
  98.3 7.7 %all-to-all-start.3 = ((bf16[16,48,256]{2,1,0:T(8,128)(2,1)}), bf16[16,48,256]{2,1,0:T(8,128)(2,1)S(1)}, u32[]{:S(2)}, u32[]{:S(2)}) async-start(bf16[16,48,256]{2,1,0:T(8,128)(2,1)} %softmax.1), calls=%async_computation.3 | async-start | bytes 786432 | tf_op jit(solution)/shard_map/all_to_all | solution.py:247
  106.0 1.9 %collective-permute-start.7 = (bf16[4,512,128]{2,1,0:T(8,128)(2,1)S(1)}, bf16[4,512,128]{2,1,0:T(8,128)(2,1)S(1)}, u32[]{:S(2)}, u32[]{:S(2)}) collective-permute-start(bf16[4,512,128]{2,1,0:T(8,128)(2,1)S(1)} %pad_maximum_fusion.own_b), channel_id=1, source_target_pairs={{0,64},{64,0},{1,65},{65,1},{2,66},{66,2},{3,67},{67,3},{4,68},{68... | collective-permute-start | bytes 1572872 | tf_op jit(solution)/shard_map/ppermute | solution.py:192
  108.0 1.9 %collective-permute-done.7.other_b = bf16[4,512,128]{2,1,0:T(8,128)(2,1)S(1)} collective-permute-done((bf16[4,512,128]{2,1,0:T(8,128)(2,1)S(1)}, bf16[4,512,128]{2,1,0:T(8,128)(2,1)S(1)}, u32[]{:S(2)}, u32[]{:S(2)}) %collective-permute-start.7) | collective-permute-done | bytes 524320 | tf_op jit(solution)/shard_map/ppermute | solution.py:192
  110.7 17.5 %all-to-all-done.3.p_ref = bf16[16,48,256]{2,1,0:T(8,128)(2,1)S(1)} async-done(((bf16[16,48,256]{2,1,0:T(8,128)(2,1)}), bf16[16,48,256]{2,1,0:T(8,128)(2,1)S(1)}, u32[]{:S(2)}, u32[]{:S(2)}) %all-to-all-start.3) | async-done | bytes 393248 | tf_op jit(solution)/shard_map/all_to_all | solution.py:247
  128.2 1.1 copy-done.4
  129.8 14.2 %all_to_all.25.c_ref = bf16[4,256,384]{2,1,0:T(8,128)(2,1)S(1)} all-to-all(bf16[4,256,384]{2,1,0:T(8,128)(2,1)S(1)} %context.1), channel_id=1, replica_groups=mesh['y'=4,'core'=2,'x'=4,'z'=16] {'x'}, dimensions={0} | all-to-all | bytes 1572864 | tf_op jit(solution)/shard_map/all_to_all | solution.py:253
  144.0 1.7 %mix.1 = bf16[2,256,768]{2,1,0:T(8,128)(2,1)} custom-call(s32[1]{0:T(128)S(6)} %copy.8.tally, bf16[4,256,384]{2,1,0:T(8,128)(2,1)S(1)} %all_to_all.25.c_ref, bf16[768,768]{1,0:T(8,128)(2,1)S(1)} %unpack_out.1.w_ref), custom_call_target="tpu_custom_call" | custom-call | flops 1073741824 | bytes 1048576 | tf_op jit(solution)/shard_map/mix/pallas_call | solution.py:254
  (20 shorter events, 6.9 us)
Async XLA Ops:
  3.3 26.2 %collective-permute-start = (bf16[512,768]{1,0:T(8,128)(2,1)}, bf16[512,768]{1,0:T(8,128)(2,1)S(1)}, u32[]{:S(2)}, u32[]{:S(2)}) collective-permute-start(bf16[512,768]{1,0:T(8,128)(2,1)} %get-tuple-element.28.x0), channel_id=1, source_target_pairs={{0,16},{16,32},{32,48},{48,0},{1,17},{17,33},{33,49},{49,1},{2,18}... | collective-permute-start | bytes 2359304 | tf_op jit(solution)/shard_map/ppermute | solution.py:192
  6.7 38.0 %all-to-all-start = ((bf16[64,16,128]{2,1,0:T(8,128)(2,1)}), bf16[64,16,128]{2,1,0:T(8,128)(2,1)S(1)}, u32[]{:S(2)}, u32[]{:S(2)}) async-start(bf16[64,16,128]{2,1,0:T(8,128)(2,1)} %get-tuple-element.26), calls=%async_computation | async-start | bytes 524288 | tf_op jit(solution)/shard_map/all_to_all | solution.py:210
  24.7 25.4 %collective-permute-start.1 = (bf16[512,768]{1,0:T(8,128)(2,1)}, bf16[512,768]{1,0:T(8,128)(2,1)S(1)}, u32[]{:S(2)}, u32[]{:S(2)}) collective-permute-start(bf16[512,768]{1,0:T(8,128)(2,1)} %get-tuple-element.28.x0), channel_id=1, source_target_pairs={{0,48},{16,0},{32,16},{48,32},{1,49},{17,1},{33,17},{49,33},{2,50}... | collective-permute-start | bytes 2359304 | tf_op jit(solution)/shard_map/ppermute | solution.py:192
  29.5 29.0 %collective-permute-start.2 = (bf16[512,768]{1,0:T(8,128)(2,1)S(1)}, bf16[512,768]{1,0:T(8,128)(2,1)}, u32[]{:S(2)}, u32[]{:S(2)}) collective-permute-start(bf16[512,768]{1,0:T(8,128)(2,1)S(1)} %collective-permute-done.x1), channel_id=1, source_target_pairs={{0,16},{16,32},{32,48},{48,0},{1,17},{17,33},{33,49},{49,1},{2,18}... | collective-permute-start | bytes 2359304 | tf_op jit(solution)/shard_map/ppermute | solution.py:192
  45.6 12.9 %all-to-all-start.1 = ((bf16[4,64,8,128]{3,2,1,0:T(8,128)(2,1)}), bf16[4,64,8,128]{3,2,1,0:T(8,128)(2,1)S(1)}, u32[]{:S(2)}, u32[]{:S(2)}) async-start(bf16[4,64,8,128]{3,2,1,0:T(8,128)(2,1)} %get-tuple-element.29), calls=%async_computation.1 | async-start | bytes 1048576 | tf_op jit(solution)/shard_map/all_to_all | solution.py:220
  50.1 13.2 %copy-start = (bf16[512,768]{1,0:T(8,128)(2,1)S(1)}, bf16[512,768]{1,0:T(8,128)(2,1)}, u32[]{:S(2)}) copy-start(bf16[512,768]{1,0:T(8,128)(2,1)} %get-tuple-element.28.x0) | copy-start | bytes 2359300
  50.1 0.9 copy-start.1
  58.5 4.8 %copy-start.2 = (bf16[512,768]{1,0:T(8,128)(2,1)S(1)}, bf16[512,768]{1,0:T(8,128)(2,1)}, u32[]{:S(2)}) copy-start(bf16[512,768]{1,0:T(8,128)(2,1)} %copy-done.1) | copy-start | bytes 2359300
  58.5 3.9 %collective-permute-start.3 = (bf16[4,64,8,128]{3,2,1,0:T(8,128)(2,1)S(1)}, bf16[4,64,8,128]{3,2,1,0:T(8,128)(2,1)S(1)}, u32[]{:S(2)}, u32[]{:S(2)}) collective-permute-start(bf16[4,64,8,128]{3,2,1,0:T(8,128)(2,1)S(1)} %all-to-all-done.1), channel_id=1, source_target_pairs={{0,64},{64,0},{1,65},{65,1},{2,66},{66,2},{3,67},{67,3},{4,68},{68... | collective-permute-start | bytes 1572872 | tf_op jit(solution)/shard_map/ppermute | solution.py:192
  68.5 0.9 copy-start.3
  69.4 27.9 %all-to-all-start.2 = ((bf16[16,48,256]{2,1,0:T(8,128)(2,1)}), bf16[16,48,256]{2,1,0:T(8,128)(2,1)S(1)}, u32[]{:S(2)}, u32[]{:S(2)}) async-start(bf16[16,48,256]{2,1,0:T(8,128)(2,1)} %get-tuple-element.35), calls=%async_computation.2 | async-start | bytes 786432 | tf_op jit(solution)/shard_map/all_to_all | solution.py:241
  74.8 10.7 %collective-permute-start.6 = (bf16[512,128]{1,0:T(8,128)(2,1)S(1)}, bf16[512,128]{1,0:T(8,128)(2,1)S(1)}, u32[]{:S(2)}, u32[]{:S(2)}) collective-permute-start(bf16[512,128]{1,0:T(8,128)(2,1)S(1)} %get-tuple-element.38), channel_id=1, source_target_pairs={{0,256},{128,384},{256,0},{384,128},{1,257},{129,385},{257,1},{385... | collective-permute-start | bytes 393224 | tf_op jit(solution)/shard_map/ppermute | solution.py:192
  79.6 6.9 %collective-permute-start.5 = (bf16[512,128]{1,0:T(8,128)(2,1)S(1)}, bf16[512,128]{1,0:T(8,128)(2,1)S(1)}, u32[]{:S(2)}, u32[]{:S(2)}) collective-permute-start(bf16[512,128]{1,0:T(8,128)(2,1)S(1)} %get-tuple-element.38), channel_id=1, source_target_pairs={{0,384},{128,0},{256,128},{384,256},{1,385},{129,1},{257,129},{385... | collective-permute-start | bytes 393224 | tf_op jit(solution)/shard_map/ppermute | solution.py:192
  82.6 8.1 %collective-permute-start.4 = (bf16[512,128]{1,0:T(8,128)(2,1)S(1)}, bf16[512,128]{1,0:T(8,128)(2,1)S(1)}, u32[]{:S(2)}, u32[]{:S(2)}) collective-permute-start(bf16[512,128]{1,0:T(8,128)(2,1)S(1)} %get-tuple-element.38), channel_id=1, source_target_pairs={{0,128},{128,256},{256,384},{384,0},{1,129},{129,257},{257,385},{3... | collective-permute-start | bytes 393224 | tf_op jit(solution)/shard_map/ppermute | solution.py:192
  98.3 29.9 %all-to-all-start.3 = ((bf16[16,48,256]{2,1,0:T(8,128)(2,1)}), bf16[16,48,256]{2,1,0:T(8,128)(2,1)S(1)}, u32[]{:S(2)}, u32[]{:S(2)}) async-start(bf16[16,48,256]{2,1,0:T(8,128)(2,1)} %softmax.1), calls=%async_computation.3 | async-start | bytes 786432 | tf_op jit(solution)/shard_map/all_to_all | solution.py:247
  106.0 3.8 %collective-permute-start.7 = (bf16[4,512,128]{2,1,0:T(8,128)(2,1)S(1)}, bf16[4,512,128]{2,1,0:T(8,128)(2,1)S(1)}, u32[]{:S(2)}, u32[]{:S(2)}) collective-permute-start(bf16[4,512,128]{2,1,0:T(8,128)(2,1)S(1)} %pad_maximum_fusion.own_b), channel_id=1, source_target_pairs={{0,64},{64,0},{1,65},{65,1},{2,66},{66,2},{3,67},{67,3},{4,68},{68... | collective-permute-start | bytes 1572872 | tf_op jit(solution)/shard_map/ppermute | solution.py:192
  128.2 1.1 copy-start.4

commit v3 on v2

--- a/solution.py
+++ b/solution.py
@@ -137,20 +137,17 @@
     return jnp.concatenate([array[:L, start : start + HD], array[L:, start : start + HD]], axis=1)
 
 
-def logits_body(x0, x1, x2, x3, w_ref, s_ref, v_ref, total):
+def logits_body(x0, x1, x2, x3, w_ref, s_ref, v_ref, q_ref, k_ref):
     for g, x_ref in enumerate((x0, x1, x2, x3)):
         made = jnp.dot(x_ref[...], w_ref[...], preferred_element_type=F32).astype(BF)
+        place = slice(128 * g, 128 * g + 128)
         for h in range(HX):
-            q = side_by_side(made, h * HD)
-            k = side_by_side(made, WX + h * HD)
-            v_ref[h, :, 128 * g : 128 * g + 128] = side_by_side(made, 2 * WX + h * HD)
-            s = lax.dot_general(q, k, (((1,), (1,)), ((), ())), preferred_element_type=F32)
-            if g == 0:
-                total[h] = s
-            elif g < 3:
-                total[h] += s
-            else:
-                s_ref[:, 16 * h : 16 * h + 16, :] = (total[h] + s).astype(BF).reshape(NZ, 16, L)
+            q_ref[h, :, place] = side_by_side(made, h * HD)
+            k_ref[h, :, place] = side_by_side(made, WX + h * HD)
+            v_ref[h, :, place] = side_by_side(made, 2 * WX + h * HD)
+    for h in range(HX):
+        s = lax.dot_general(q_ref[h], k_ref[h], (((1,), (1,)), ((), ())), preferred_element_type=F32)
+        s_ref[:, 16 * h : 16 * h + 16, :] = s.astype(BF).reshape(NZ, 16, L)
 
 
 def softmax_body(count_ref, s_ref, p_ref):
@@ -175,12 +172,16 @@
             c_ref[to, :, 128 * h : 128 * h + 128] = made[:, 128 * g : 128 * g + 128]
 
 
-def mixed_body(tally, c_ref, w_ref, out_ref):
+def mixed_body(tally, c_ref, w_ref, out_hbm, made_ref, sems):
     chunks = [c_ref[h // HX, :, 128 * (h % HX) : 128 * (h % HX) + 128] for h in range(HEADS)]
-    for r in range(2):
+    copies = [pltpu.make_async_copy(made_ref.at[r], out_hbm.at[r], sems.at[r]) for r in range(2)]
+    for r, copy in enumerate(copies):
         a = jnp.concatenate([chunk[:, HD * r : HD * r + HD] for chunk in chunks], axis=1)
         made = jnp.dot(a, w_ref[...], preferred_element_type=F32)
-        out_ref[r] = (made * (r < tally[0]).astype(F32)).astype(BF)
+        made_ref[r] = (made * (r < tally[0]).astype(F32)).astype(BF)
+        copy.start()
+    for copy in copies:
+        copy.wait()
 
 
 def struct(shape, dtype=BF):
@@ -230,28 +231,26 @@
         logits_body,
         (struct((NZ, 16 * HX, L)), struct((HX, L, 8 * HD))),
         [VMEM] * 5,
-        [pltpu.VMEM((HX, L, L), F32)],
+        [pltpu.VMEM((HX, L, 8 * HD), BF)] * 2,
         flops=3 << 30,
         nbytes=1 << 23,
         name="logits",
     )(normed, near, far, across, w_in)
 
     s, late = fence(s, late)
-    lates = [late] + [shift(late, "y", NY, d) for d in (1, -1, 2)]
-    s = lax.all_to_all(s, "z", 0, 0, tiled=True)
-    s, *lates = fence(s, *lates)
-    p = call(softmax_body, struct((NZ, 16 * HX, L)), [VMEM, VMEM], flops=1 << 20, name="softmax")(count, s)
-    own_late = jnp.stack(lates)
-    p, own_late = fence(p, own_late)
+    own_late = jnp.stack([late] + [shift(late, "y", NY, d) for d in (1, -1, 2)])
     other_late = shift(own_late, "core", 2, 1)
-    p = lax.all_to_all(p, "z", 0, 0, tiled=True)
     w_out = call(out_body, struct((D, D)), [SMEM] + [VMEM] * 4, [held, held, wide], 1 << 20, 1 << 22, name="unpack_out")(
         me, own, other, own_late, other_late
     )
-    p, w_out = fence(p, w_out)
+    s = lax.all_to_all(s, "z", 0, 0, tiled=True)
+    s, w_out = fence(s, w_out)
+    p = call(softmax_body, struct((NZ, 16 * HX, L)), [VMEM, VMEM], flops=1 << 20, name="softmax")(count, s)
+    p = lax.all_to_all(p, "z", 0, 0, tiled=True)
     c = call(context_body, struct((NX, L, 2 * WX)), [SMEM, VMEM, ANY], flops=1 << 29, name="context")(me, p, v)
     c = lax.all_to_all(c, "x", 0, 0, tiled=True)
-    return call(mixed_body, struct((2, L, D)), [SMEM, VMEM, VMEM], flops=1 << 30, name="mix")(tally, c, w_out)
+    scratch = [pltpu.VMEM((2, L, D), BF), pltpu.SemaphoreType.DMA((2,))]
+    return call(mixed_body, struct((2, L, D)), [SMEM, VMEM, VMEM], scratch, 1 << 30, name="mix", outs=HBM)(tally, c, w_out)
 
 
 def solution(mesh):

time: 146 us -> 146 us (level)
  blocking collectives: 14.2 us -> 46.4 us
  waiting for transfers between devices: 53.8 us -> 31.5 us
  starting transfers between devices: 60.3 us -> 52.6 us
    all_to_all x0 -> x1, blocking collectives: none -> 32.3 us  [per_device(): p = lax.all_to_all(p, 'z', 0, 0, tiled=True)]
    all_to_all x1 -> x0, waiting for transfers between devices: 17.5 us -> none  [per_device(): p = lax.all_to_all(p, 'z', 0, 0, tiled=True)]
    all_to_all x1 -> x0, starting transfers between devices: 7.71 us -> none  [per_device(): p = lax.all_to_all(p, 'z', 0, 0, tiled=True)]
    all_to_all x1, waiting for transfers between devices: 6.53 us -> 1.75 us  [per_device(): s = lax.all_to_all(s, 'z', 0, 0, tiled=True)]
  transfers between devices with their start and end apart: 12 -> 11, of which waited for: 8 -> 7; matrix products, arithmetic and copies ran while one was open for 0% -> 0% of each run, Pallas kernels for 1% -> 1%
where the time goes in v3:
time: 146 us
  starting transfers between devices  52.6 us (36%)
  blocking collectives  46.4 us (32%)
  waiting for transfers between devices  31.5 us (22%)
  Pallas kernels  12.3 us (8%)
  local copies, waits for them, and re-layouts  1.8 us (1%)
    all_to_all x1, blocking collectives, per_device(): p = lax.all_to_all(p, 'z', 0, 0, tiled=True)  32.3 us
    ppermute x8, starting transfers between devices, per_device(): lax.ppermute(a, axis, [(i, (i + d) % n) for i in range(n)])  24.7 us
    all_to_all x1, starting transfers between devices, per_device(): pieces = lax.all_to_all(pieces, ('x', 'z'), 0, 0, tiled=True)  17.9 us
    all_to_all x1, blocking collectives, per_device(): c = lax.all_to_all(c, 'x', 0, 0, tiled=True)  14.2 us
    all_to_all x1, waiting for transfers between devices, per_device(): pieces = lax.all_to_all(pieces, ('x', 'z'), 0, 0, tiled=True)  13.3 us
    ppermute x8, waiting for transfers between devices, per_device(): lax.ppermute(a, axis, [(i, (i + d) % n) for i in range(n)])  8.93 us
    all_to_all x1, waiting for transfers between devices, per_device(): own = lax.all_to_all(early, 'y', 0, 0, tiled=True)  7.51 us
    all_to_all x1, starting transfers between devices, per_device(): s = lax.all_to_all(s, 'z', 0, 0, tiled=True)  5.49 us
  transfers between devices with their start and end apart: 11, of which 7 were waited for; matrix products, arithmetic and copies ran while one was open for 0% of the time, Pallas kernels for 1%

profile of v3, /device:TPU:32, one launch (start us, length us, event | category | flops | bytes accessed | tf_op | source)
XLA Modules:
  0.0 145.5 jit_solution(2799086721141507049)
XLA Ops:
  0.7 2.7 %first.1 = (bf16[64,16,128]{2,1,0:T(8,128)(2,1)}, bf16[512,768]{1,0:T(8,128)(2,1)}) custom-call(s32[1]{0:T(128)} %bitcast.me, s32[1]{0:T(128)S(6)} %copy.8.tally, bf16[512,768]{1,0:T(8,128)(2,1)} %bitcast.13, f32[768]{0:T(1024)} %g_hbm.1, bf16[12,768]{1,0:T(8,128)(2,1)} %q_hbm.1, bf16[12,768]{1,0:T(8,128)(2,1)} %k_hbm.1, bf16[12,768]{1,0:T(8,128)(2,1)} %v_hbm.1, ...), custom_call_target="tpu_custom_call" | custom-call | bytes 1048576 | tf_op jit(solution)/shard_map/first/pallas_call | solution.py:196
  3.3 3.4 %collective-permute-start = (bf16[512,768]{1,0:T(8,128)(2,1)}, bf16[512,768]{1,0:T(8,128)(2,1)S(1)}, u32[]{:S(2)}, u32[]{:S(2)}) collective-permute-start(bf16[512,768]{1,0:T(8,128)(2,1)} %get-tuple-element.21.x0), channel_id=1, source_target_pairs={{0,16},{16,32},{32,48},{48,0},{1,17},{17,33},{33,49},{49,1},{2,18}... | collective-permute-start | bytes 2359304 | tf_op jit(solution)/shard_map/ppermute | solution.py:193
  6.7 17.9 %all-to-all-start = ((bf16[64,16,128]{2,1,0:T(8,128)(2,1)}), bf16[64,16,128]{2,1,0:T(8,128)(2,1)S(1)}, u32[]{:S(2)}, u32[]{:S(2)}) async-start(bf16[64,16,128]{2,1,0:T(8,128)(2,1)} %get-tuple-element.19), calls=%async_computation | async-start | bytes 524288 | tf_op jit(solution)/shard_map/all_to_all | solution.py:211
  24.7 4.8 %collective-permute-start.1 = (bf16[512,768]{1,0:T(8,128)(2,1)}, bf16[512,768]{1,0:T(8,128)(2,1)S(1)}, u32[]{:S(2)}, u32[]{:S(2)}) collective-permute-start(bf16[512,768]{1,0:T(8,128)(2,1)} %get-tuple-element.21.x0), channel_id=1, source_target_pairs={{0,48},{16,0},{32,16},{48,32},{1,49},{17,1},{33,17},{49,33},{2,50}... | collective-permute-start | bytes 2359304 | tf_op jit(solution)/shard_map/ppermute | solution.py:193
  29.5 1.9 %collective-permute-start.2 = (bf16[512,768]{1,0:T(8,128)(2,1)S(1)}, bf16[512,768]{1,0:T(8,128)(2,1)}, u32[]{:S(2)}, u32[]{:S(2)}) collective-permute-start(bf16[512,768]{1,0:T(8,128)(2,1)S(1)} %collective-permute-done.x1), channel_id=1, source_target_pairs={{0,16},{16,32},{32,48},{48,0},{1,17},{17,33},{33,49},{49,1},{2,18}... | collective-permute-start | bytes 2359304 | tf_op jit(solution)/shard_map/ppermute | solution.py:193
  31.4 13.3 %all-to-all-done.pieces_ref = bf16[64,16,128]{2,1,0:T(8,128)(2,1)S(1)} async-done(((bf16[64,16,128]{2,1,0:T(8,128)(2,1)}), bf16[64,16,128]{2,1,0:T(8,128)(2,1)S(1)}, u32[]{:S(2)}, u32[]{:S(2)}) %all-to-all-start) | async-done | bytes 262176 | tf_op jit(solution)/shard_map/all_to_all | solution.py:211
  45.6 4.5 %all-to-all-start.1 = ((bf16[4,64,8,128]{3,2,1,0:T(8,128)(2,1)}), bf16[4,64,8,128]{3,2,1,0:T(8,128)(2,1)S(1)}, u32[]{:S(2)}, u32[]{:S(2)}) async-start(bf16[4,64,8,128]{3,2,1,0:T(8,128)(2,1)} %get-tuple-element.22), calls=%async_computation.1 | async-start | bytes 1048576 | tf_op jit(solution)/shard_map/all_to_all | solution.py:221
  50.1 0.9 copy-done.1
  51.0 7.5 %all-to-all-done.1 = bf16[4,64,8,128]{3,2,1,0:T(8,128)(2,1)S(1)} async-done(((bf16[4,64,8,128]{3,2,1,0:T(8,128)(2,1)}), bf16[4,64,8,128]{3,2,1,0:T(8,128)(2,1)S(1)}, u32[]{:S(2)}, u32[]{:S(2)}) %all-to-all-start.1) | async-done | bytes 524320 | tf_op jit(solution)/shard_map/all_to_all | solution.py:221
  58.5 2.0 %collective-permute-start.3 = (bf16[4,64,8,128]{3,2,1,0:T(8,128)(2,1)S(1)}, bf16[4,64,8,128]{3,2,1,0:T(8,128)(2,1)S(1)}, u32[]{:S(2)}, u32[]{:S(2)}) collective-permute-start(bf16[4,64,8,128]{3,2,1,0:T(8,128)(2,1)S(1)} %all-to-all-done.1), channel_id=1, source_target_pairs={{0,64},{64,0},{1,65},{65,1},{2,66},{66,2},{3,67},{67,3},{4,68},{68... | collective-permute-start | bytes 1572872 | tf_op jit(solution)/shard_map/ppermute | solution.py:193
  60.6 1.9 %collective-permute-done.3 = bf16[4,64,8,128]{3,2,1,0:T(8,128)(2,1)S(1)} collective-permute-done((bf16[4,64,8,128]{3,2,1,0:T(8,128)(2,1)S(1)}, bf16[4,64,8,128]{3,2,1,0:T(8,128)(2,1)S(1)}, u32[]{:S(2)}, u32[]{:S(2)}) %collective-permute-start.3) | collective-permute-done | bytes 524320 | tf_op jit(solution)/shard_map/ppermute | solution.py:193
  63.3 4.8 %logits.1 = (bf16[16,48,256]{2,1,0:T(8,128)(2,1)}, bf16[3,256,512]{2,1,0:T(8,128)(2,1)S(1)}) custom-call(bf16[512,768]{1,0:T(8,128)(2,1)S(1)} %copy-done, bf16[512,768]{1,0:T(8,128)(2,1)S(1)} %collective-permute-done.x1, bf16[512,768]{1,0:T(8,128)(2,1)S(1)} %copy-done.2, bf16[512,768]{1,0:T(8,128)(2,1)} %collective-permute-done.2.x3, ...), custom_call_target="tpu_custom_call" | custom-call | flops 3221225472 | bytes 8388608 | tf_op jit(solution)/shard_map/logits/pallas_call | solution.py:230
  68.9 5.5 %all-to-all-start.2 = ((bf16[16,48,256]{2,1,0:T(8,128)(2,1)}), bf16[16,48,256]{2,1,0:T(8,128)(2,1)S(1)}, u32[]{:S(2)}, u32[]{:S(2)}) async-start(bf16[16,48,256]{2,1,0:T(8,128)(2,1)} %get-tuple-element.28), calls=%async_computation.2 | async-start | bytes 786432 | tf_op jit(solution)/shard_map/all_to_all | solution.py:246
  74.4 4.8 %collective-permute-start.6 = (bf16[512,128]{1,0:T(8,128)(2,1)S(1)}, bf16[512,128]{1,0:T(8,128)(2,1)S(1)}, u32[]{:S(2)}, u32[]{:S(2)}) collective-permute-start(bf16[512,128]{1,0:T(8,128)(2,1)S(1)} %get-tuple-element.29), channel_id=1, source_target_pairs={{0,256},{128,384},{256,0},{384,128},{1,257},{129,385},{257,1},{385... | collective-permute-start | bytes 393224 | tf_op jit(solution)/shard_map/ppermute | solution.py:193
  79.2 3.0 %collective-permute-start.5 = (bf16[512,128]{1,0:T(8,128)(2,1)S(1)}, bf16[512,128]{1,0:T(8,128)(2,1)S(1)}, u32[]{:S(2)}, u32[]{:S(2)}) collective-permute-start(bf16[512,128]{1,0:T(8,128)(2,1)S(1)} %get-tuple-element.29), channel_id=1, source_target_pairs={{0,384},{128,0},{256,128},{384,256},{1,385},{129,1},{257,129},{385... | collective-permute-start | bytes 393224 | tf_op jit(solution)/shard_map/ppermute | solution.py:193
  82.2 2.9 %collective-permute-start.4 = (bf16[512,128]{1,0:T(8,128)(2,1)S(1)}, bf16[512,128]{1,0:T(8,128)(2,1)S(1)}, u32[]{:S(2)}, u32[]{:S(2)}) collective-permute-start(bf16[512,128]{1,0:T(8,128)(2,1)S(1)} %get-tuple-element.29), channel_id=1, source_target_pairs={{0,128},{128,256},{256,384},{384,0},{1,129},{129,257},{257,385},{3... | collective-permute-start | bytes 393224 | tf_op jit(solution)/shard_map/ppermute | solution.py:193
  85.1 1.0 collective-permute-done.5
  86.1 4.2 %collective-permute-done.4 = bf16[512,128]{1,0:T(8,128)(2,1)S(1)} collective-permute-done((bf16[512,128]{1,0:T(8,128)(2,1)S(1)}, bf16[512,128]{1,0:T(8,128)(2,1)S(1)}, u32[]{:S(2)}, u32[]{:S(2)}) %collective-permute-start.4) | collective-permute-done | bytes 131104 | tf_op jit(solution)/shard_map/ppermute | solution.py:193
  90.3 1.9 %collective-permute-start.7 = (bf16[4,512,128]{2,1,0:T(8,128)(2,1)S(1)}, bf16[4,512,128]{2,1,0:T(8,128)(2,1)S(1)}, u32[]{:S(2)}, u32[]{:S(2)}) collective-permute-start(bf16[4,512,128]{2,1,0:T(8,128)(2,1)S(1)} %pad_maximum_fusion.own_b), channel_id=1, source_target_pairs={{0,64},{64,0},{1,65},{65,1},{2,66},{66,2},{3,67},{67,3},{4,68},{68... | collective-permute-start | bytes 1572872 | tf_op jit(solution)/shard_map/ppermute | solution.py:193
  92.3 1.9 %collective-permute-done.7.other_b = bf16[4,512,128]{2,1,0:T(8,128)(2,1)S(1)} collective-permute-done((bf16[4,512,128]{2,1,0:T(8,128)(2,1)S(1)}, bf16[4,512,128]{2,1,0:T(8,128)(2,1)S(1)}, u32[]{:S(2)}, u32[]{:S(2)}) %collective-permute-start.7) | collective-permute-done | bytes 524320 | tf_op jit(solution)/shard_map/ppermute | solution.py:193
  95.0 1.8 %all-to-all-done.2.s_ref = bf16[16,48,256]{2,1,0:T(8,128)(2,1)S(1)} async-done(((bf16[16,48,256]{2,1,0:T(8,128)(2,1)}), bf16[16,48,256]{2,1,0:T(8,128)(2,1)S(1)}, u32[]{:S(2)}, u32[]{:S(2)}) %all-to-all-start.2) | async-done | bytes 393248 | tf_op jit(solution)/shard_map/all_to_all | solution.py:246
  97.1 32.3 %all_to_all.25.p_ref = bf16[16,48,256]{2,1,0:T(8,128)(2,1)S(1)} all-to-all(bf16[16,48,256]{2,1,0:T(8,128)(2,1)S(1)} %softmax.1), channel_id=1, replica_groups=mesh['y'=4,'core'=2,'x'=4,'z'=16] {'z'}, dimensions={0} | all-to-all | bytes 786432 | tf_op jit(solution)/shard_map/all_to_all | solution.py:249
  129.8 14.2 %all_to_all.26.c_ref = bf16[4,256,384]{2,1,0:T(8,128)(2,1)S(1)} all-to-all(bf16[4,256,384]{2,1,0:T(8,128)(2,1)S(1)} %context.1), channel_id=1, replica_groups=mesh['y'=4,'core'=2,'x'=4,'z'=16] {'x'}, dimensions={0} | all-to-all | bytes 1572864 | tf_op jit(solution)/shard_map/all_to_all | solution.py:251
  143.9 1.6 %mix.1 = bf16[2,256,768]{2,1,0:T(8,128)(2,1)} custom-call(s32[1]{0:T(128)S(6)} %copy.8.tally, bf16[4,256,384]{2,1,0:T(8,128)(2,1)S(1)} %all_to_all.26.c_ref, bf16[768,768]{1,0:T(8,128)(2,1)S(1)} %unpack_out.1.w_ref), custom_call_target="tpu_custom_call" | custom-call | flops 1073741824 | bytes 1048576 | tf_op jit(solution)/shard_map/mix/pallas_call | solution.py:253
  (19 shorter events, 4.3 us)
Async XLA Ops:
  3.3 26.2 %collective-permute-start = (bf16[512,768]{1,0:T(8,128)(2,1)}, bf16[512,768]{1,0:T(8,128)(2,1)S(1)}, u32[]{:S(2)}, u32[]{:S(2)}) collective-permute-start(bf16[512,768]{1,0:T(8,128)(2,1)} %get-tuple-element.21.x0), channel_id=1, source_target_pairs={{0,16},{16,32},{32,48},{48,0},{1,17},{17,33},{33,49},{49,1},{2,18}... | collective-permute-start | bytes 2359304 | tf_op jit(solution)/shard_map/ppermute | solution.py:193
  6.7 38.0 %all-to-all-start = ((bf16[64,16,128]{2,1,0:T(8,128)(2,1)}), bf16[64,16,128]{2,1,0:T(8,128)(2,1)S(1)}, u32[]{:S(2)}, u32[]{:S(2)}) async-start(bf16[64,16,128]{2,1,0:T(8,128)(2,1)} %get-tuple-element.19), calls=%async_computation | async-start | bytes 524288 | tf_op jit(solution)/shard_map/all_to_all | solution.py:211
  24.7 25.4 %collective-permute-start.1 = (bf16[512,768]{1,0:T(8,128)(2,1)}, bf16[512,768]{1,0:T(8,128)(2,1)S(1)}, u32[]{:S(2)}, u32[]{:S(2)}) collective-permute-start(bf16[512,768]{1,0:T(8,128)(2,1)} %get-tuple-element.21.x0), channel_id=1, source_target_pairs={{0,48},{16,0},{32,16},{48,32},{1,49},{17,1},{33,17},{49,33},{2,50}... | collective-permute-start | bytes 2359304 | tf_op jit(solution)/shard_map/ppermute | solution.py:193
  29.5 29.0 %collective-permute-start.2 = (bf16[512,768]{1,0:T(8,128)(2,1)S(1)}, bf16[512,768]{1,0:T(8,128)(2,1)}, u32[]{:S(2)}, u32[]{:S(2)}) collective-permute-start(bf16[512,768]{1,0:T(8,128)(2,1)S(1)} %collective-permute-done.x1), channel_id=1, source_target_pairs={{0,16},{16,32},{32,48},{48,0},{1,17},{17,33},{33,49},{49,1},{2,18}... | collective-permute-start | bytes 2359304 | tf_op jit(solution)/shard_map/ppermute | solution.py:193
  45.6 12.9 %all-to-all-start.1 = ((bf16[4,64,8,128]{3,2,1,0:T(8,128)(2,1)}), bf16[4,64,8,128]{3,2,1,0:T(8,128)(2,1)S(1)}, u32[]{:S(2)}, u32[]{:S(2)}) async-start(bf16[4,64,8,128]{3,2,1,0:T(8,128)(2,1)} %get-tuple-element.22), calls=%async_computation.1 | async-start | bytes 1048576 | tf_op jit(solution)/shard_map/all_to_all | solution.py:221
  50.1 13.2 %copy-start = (bf16[512,768]{1,0:T(8,128)(2,1)S(1)}, bf16[512,768]{1,0:T(8,128)(2,1)}, u32[]{:S(2)}) copy-start(bf16[512,768]{1,0:T(8,128)(2,1)} %get-tuple-element.21.x0) | copy-start | bytes 2359300
  50.1 0.9 copy-start.1
  58.5 4.8 %copy-start.2 = (bf16[512,768]{1,0:T(8,128)(2,1)S(1)}, bf16[512,768]{1,0:T(8,128)(2,1)}, u32[]{:S(2)}) copy-start(bf16[512,768]{1,0:T(8,128)(2,1)} %copy-done.1) | copy-start | bytes 2359300
  58.5 3.9 %collective-permute-start.3 = (bf16[4,64,8,128]{3,2,1,0:T(8,128)(2,1)S(1)}, bf16[4,64,8,128]{3,2,1,0:T(8,128)(2,1)S(1)}, u32[]{:S(2)}, u32[]{:S(2)}) collective-permute-start(bf16[4,64,8,128]{3,2,1,0:T(8,128)(2,1)S(1)} %all-to-all-done.1), channel_id=1, source_target_pairs={{0,64},{64,0},{1,65},{65,1},{2,66},{66,2},{3,67},{67,3},{4,68},{68... | collective-permute-start | bytes 1572872 | tf_op jit(solution)/shard_map/ppermute | solution.py:193
  68.1 0.9 copy-start.3
  68.9 27.9 %all-to-all-start.2 = ((bf16[16,48,256]{2,1,0:T(8,128)(2,1)}), bf16[16,48,256]{2,1,0:T(8,128)(2,1)S(1)}, u32[]{:S(2)}, u32[]{:S(2)}) async-start(bf16[16,48,256]{2,1,0:T(8,128)(2,1)} %get-tuple-element.28), calls=%async_computation.2 | async-start | bytes 786432 | tf_op jit(solution)/shard_map/all_to_all | solution.py:246
  74.4 10.7 %collective-permute-start.6 = (bf16[512,128]{1,0:T(8,128)(2,1)S(1)}, bf16[512,128]{1,0:T(8,128)(2,1)S(1)}, u32[]{:S(2)}, u32[]{:S(2)}) collective-permute-start(bf16[512,128]{1,0:T(8,128)(2,1)S(1)} %get-tuple-element.29), channel_id=1, source_target_pairs={{0,256},{128,384},{256,0},{384,128},{1,257},{129,385},{257,1},{385... | collective-permute-start | bytes 393224 | tf_op jit(solution)/shard_map/ppermute | solution.py:193
  79.2 6.9 %collective-permute-start.5 = (bf16[512,128]{1,0:T(8,128)(2,1)S(1)}, bf16[512,128]{1,0:T(8,128)(2,1)S(1)}, u32[]{:S(2)}, u32[]{:S(2)}) collective-permute-start(bf16[512,128]{1,0:T(8,128)(2,1)S(1)} %get-tuple-element.29), channel_id=1, source_target_pairs={{0,384},{128,0},{256,128},{384,256},{1,385},{129,1},{257,129},{385... | collective-permute-start | bytes 393224 | tf_op jit(solution)/shard_map/ppermute | solution.py:193
  82.2 8.1 %collective-permute-start.4 = (bf16[512,128]{1,0:T(8,128)(2,1)S(1)}, bf16[512,128]{1,0:T(8,128)(2,1)S(1)}, u32[]{:S(2)}, u32[]{:S(2)}) collective-permute-start(bf16[512,128]{1,0:T(8,128)(2,1)S(1)} %get-tuple-element.29), channel_id=1, source_target_pairs={{0,128},{128,256},{256,384},{384,0},{1,129},{129,257},{257,385},{3... | collective-permute-start | bytes 393224 | tf_op jit(solution)/shard_map/ppermute | solution.py:193
  90.3 3.8 %collective-permute-start.7 = (bf16[4,512,128]{2,1,0:T(8,128)(2,1)S(1)}, bf16[4,512,128]{2,1,0:T(8,128)(2,1)S(1)}, u32[]{:S(2)}, u32[]{:S(2)}) collective-permute-start(bf16[4,512,128]{2,1,0:T(8,128)(2,1)S(1)} %pad_maximum_fusion.own_b), channel_id=1, source_target_pairs={{0,64},{64,0},{1,65},{65,1},{2,66},{66,2},{3,67},{67,3},{4,68},{68... | collective-permute-start | bytes 1572872 | tf_op jit(solution)/shard_map/ppermute | solution.py:193
  95.0 34.3 %copy-start.4 = (bf16[3,256,512]{2,1,0:T(8,128)(2,1)S(1)}, bf16[3,256,512]{2,1,0:T(8,128)(2,1)}, u32[]{:S(2)}) copy-start(bf16[3,256,512]{2,1,0:T(8,128)(2,1)} %copy-done.3) | copy-start | bytes 2359300

commit v4 on v3

--- a/solution.py
+++ b/solution.py
@@ -237,16 +237,16 @@
         name="logits",
     )(normed, near, far, across, w_in)
 
-    s, late = fence(s, late)
+    s = lax.all_to_all(s, "z", 0, 0, tiled=True)
+    p = call(softmax_body, struct((NZ, 16 * HX, L)), [VMEM, VMEM], flops=1 << 20, name="softmax")(count, s)
+    p, late = fence(p, late)
     own_late = jnp.stack([late] + [shift(late, "y", NY, d) for d in (1, -1, 2)])
     other_late = shift(own_late, "core", 2, 1)
     w_out = call(out_body, struct((D, D)), [SMEM] + [VMEM] * 4, [held, held, wide], 1 << 20, 1 << 22, name="unpack_out")(
         me, own, other, own_late, other_late
     )
-    s = lax.all_to_all(s, "z", 0, 0, tiled=True)
-    s, w_out = fence(s, w_out)
-    p = call(softmax_body, struct((NZ, 16 * HX, L)), [VMEM, VMEM], flops=1 << 20, name="softmax")(count, s)
     p = lax.all_to_all(p, "z", 0, 0, tiled=True)
+    p, w_out = fence(p, w_out)
     c = call(context_body, struct((NX, L, 2 * WX)), [SMEM, VMEM, ANY], flops=1 << 29, name="context")(me, p, v)
     c = lax.all_to_all(c, "x", 0, 0, tiled=True)
     scratch = [pltpu.VMEM((2, L, D), BF), pltpu.SemaphoreType.DMA((2,))]

time: 146 us -> 143 us (0.979)
  blocking collectives: 46.4 us -> 41.9 us
  starting transfers between devices: 52.6 us -> 54.9 us
    all_to_all x1, blocking collectives: 32.3 us -> 27.7 us  [per_device(): s = lax.all_to_all(s, 'z', 0, 0, tiled=True)]
    all_to_all x1, starting transfers between devices: 5.49 us -> 7.7 us  [per_device(): p = lax.all_to_all(p, 'z', 0, 0, tiled=True)]
where the time goes in v4:
time: 143 us
  starting transfers between devices  54.9 us (38%)
  blocking collectives  41.9 us (29%)
  waiting for transfers between devices  32 us (22%)
  Pallas kernels  12.3 us (9%)
    all_to_all x1, blocking collectives, per_device(): s = lax.all_to_all(s, 'z', 0, 0, tiled=True)  27.7 us
    ppermute x8, starting transfers between devices, per_device(): lax.ppermute(a, axis, [(i, (i + d) % n) for i in range(n)])  24.9 us
    all_to_all x1, starting transfers between devices, per_device(): pieces = lax.all_to_all(pieces, ('x', 'z'), 0, 0, tiled=True)  17.9 us
    all_to_all x1, blocking collectives, per_device(): c = lax.all_to_all(c, 'x', 0, 0, tiled=True)  14.2 us
    all_to_all x1, waiting for transfers between devices, per_device(): pieces = lax.all_to_all(pieces, ('x', 'z'), 0, 0, tiled=True)  13.3 us
    ppermute x8, waiting for transfers between devices, per_device(): lax.ppermute(a, axis, [(i, (i + d) % n) for i in range(n)])  8.93 us
    all_to_all x1, waiting for transfers between devices, per_device(): own = lax.all_to_all(early, 'y', 0, 0, tiled=True)  8.42 us
    all_to_all x1, starting transfers between devices, per_device(): p = lax.all_to_all(p, 'z', 0, 0, tiled=True)  7.7 us
  transfers between devices with their start and end apart: 11, of which 7 were waited for; matrix products, arithmetic and copies ran while one was open for 0% of the time, Pallas kernels for 1%

profile of v4, /device:TPU:32, one launch (start us, length us, event | category | flops | bytes accessed | tf_op | source)
XLA Modules:
  0.0 142.8 jit_solution(15666731102986836027)
XLA Ops:
  0.7 2.7 %first.1 = (bf16[64,16,128]{2,1,0:T(8,128)(2,1)}, bf16[512,768]{1,0:T(8,128)(2,1)}) custom-call(s32[1]{0:T(128)} %bitcast.me, s32[1]{0:T(128)S(6)} %copy.8.tally, bf16[512,768]{1,0:T(8,128)(2,1)} %bitcast.13, f32[768]{0:T(1024)} %g_hbm.1, bf16[12,768]{1,0:T(8,128)(2,1)} %q_hbm.1, bf16[12,768]{1,0:T(8,128)(2,1)} %k_hbm.1, bf16[12,768]{1,0:T(8,128)(2,1)} %v_hbm.1, ...), custom_call_target="tpu_custom_call" | custom-call | bytes 1048576 | tf_op jit(solution)/shard_map/first/pallas_call | solution.py:196
  3.3 3.4 %collective-permute-start = (bf16[512,768]{1,0:T(8,128)(2,1)}, bf16[512,768]{1,0:T(8,128)(2,1)S(1)}, u32[]{:S(2)}, u32[]{:S(2)}) collective-permute-start(bf16[512,768]{1,0:T(8,128)(2,1)} %get-tuple-element.21.x0), channel_id=1, source_target_pairs={{0,16},{16,32},{32,48},{48,0},{1,17},{17,33},{33,49},{49,1},{2,18}... | collective-permute-start | bytes 2359304 | tf_op jit(solution)/shard_map/ppermute | solution.py:193
  6.7 17.9 %all-to-all-start = ((bf16[64,16,128]{2,1,0:T(8,128)(2,1)}), bf16[64,16,128]{2,1,0:T(8,128)(2,1)S(1)}, u32[]{:S(2)}, u32[]{:S(2)}) async-start(bf16[64,16,128]{2,1,0:T(8,128)(2,1)} %get-tuple-element.19), calls=%async_computation | async-start | bytes 524288 | tf_op jit(solution)/shard_map/all_to_all | solution.py:211
  24.7 4.8 %collective-permute-start.1 = (bf16[512,768]{1,0:T(8,128)(2,1)}, bf16[512,768]{1,0:T(8,128)(2,1)S(1)}, u32[]{:S(2)}, u32[]{:S(2)}) collective-permute-start(bf16[512,768]{1,0:T(8,128)(2,1)} %get-tuple-element.21.x0), channel_id=1, source_target_pairs={{0,48},{16,0},{32,16},{48,32},{1,49},{17,1},{33,17},{49,33},{2,50}... | collective-permute-start | bytes 2359304 | tf_op jit(solution)/shard_map/ppermute | solution.py:193
  29.5 1.9 %collective-permute-start.2 = (bf16[512,768]{1,0:T(8,128)(2,1)S(1)}, bf16[512,768]{1,0:T(8,128)(2,1)}, u32[]{:S(2)}, u32[]{:S(2)}) collective-permute-start(bf16[512,768]{1,0:T(8,128)(2,1)S(1)} %collective-permute-done.x1), channel_id=1, source_target_pairs={{0,16},{16,32},{32,48},{48,0},{1,17},{17,33},{33,49},{49,1},{2,18}... | collective-permute-start | bytes 2359304 | tf_op jit(solution)/shard_map/ppermute | solution.py:193
  31.4 13.3 %all-to-all-done.pieces_ref = bf16[64,16,128]{2,1,0:T(8,128)(2,1)S(1)} async-done(((bf16[64,16,128]{2,1,0:T(8,128)(2,1)}), bf16[64,16,128]{2,1,0:T(8,128)(2,1)S(1)}, u32[]{:S(2)}, u32[]{:S(2)}) %all-to-all-start) | async-done | bytes 262176 | tf_op jit(solution)/shard_map/all_to_all | solution.py:211
  45.6 4.5 %all-to-all-start.1 = ((bf16[4,64,8,128]{3,2,1,0:T(8,128)(2,1)}), bf16[4,64,8,128]{3,2,1,0:T(8,128)(2,1)S(1)}, u32[]{:S(2)}, u32[]{:S(2)}) async-start(bf16[4,64,8,128]{3,2,1,0:T(8,128)(2,1)} %get-tuple-element.22), calls=%async_computation.1 | async-start | bytes 1048576 | tf_op jit(solution)/shard_map/all_to_all | solution.py:221
  50.1 8.4 %all-to-all-done.1 = bf16[4,64,8,128]{3,2,1,0:T(8,128)(2,1)S(1)} async-done(((bf16[4,64,8,128]{3,2,1,0:T(8,128)(2,1)}), bf16[4,64,8,128]{3,2,1,0:T(8,128)(2,1)S(1)}, u32[]{:S(2)}, u32[]{:S(2)}) %all-to-all-start.1) | async-done | bytes 524320 | tf_op jit(solution)/shard_map/all_to_all | solution.py:221
  58.5 1.9 %collective-permute-start.3 = (bf16[4,64,8,128]{3,2,1,0:T(8,128)(2,1)S(1)}, bf16[4,64,8,128]{3,2,1,0:T(8,128)(2,1)S(1)}, u32[]{:S(2)}, u32[]{:S(2)}) collective-permute-start(bf16[4,64,8,128]{3,2,1,0:T(8,128)(2,1)S(1)} %all-to-all-done.1), channel_id=1, source_target_pairs={{0,64},{64,0},{1,65},{65,1},{2,66},{66,2},{3,67},{67,3},{4,68},{68... | collective-permute-start | bytes 1572872 | tf_op jit(solution)/shard_map/ppermute | solution.py:193
  60.4 1.9 %collective-permute-done.3 = bf16[4,64,8,128]{3,2,1,0:T(8,128)(2,1)S(1)} collective-permute-done((bf16[4,64,8,128]{3,2,1,0:T(8,128)(2,1)S(1)}, bf16[4,64,8,128]{3,2,1,0:T(8,128)(2,1)S(1)}, u32[]{:S(2)}, u32[]{:S(2)}) %collective-permute-start.3) | collective-permute-done | bytes 524320 | tf_op jit(solution)/shard_map/ppermute | solution.py:193
  63.1 4.0 %logits.1 = (bf16[16,48,256]{2,1,0:T(8,128)(2,1)S(1)}, bf16[3,256,512]{2,1,0:T(8,128)(2,1)S(1)}) custom-call(bf16[512,768]{1,0:T(8,128)(2,1)S(1)} %copy-done, bf16[512,768]{1,0:T(8,128)(2,1)S(1)} %collective-permute-done.x1, bf16[512,768]{1,0:T(8,128)(2,1)S(1)} %collective-permute-done.1.x2, bf16[512,768]{1,0:T(8,128)(2,1)} %collective-permute-done.2.x3, ...), custom_call_target="tpu_custom_call" | custom-call | flops 3221225472 | bytes 8388608 | tf_op jit(solution)/shard_map/logits/pallas_call | solution.py:230
  68.0 27.7 %all_to_all.25.s_ref = bf16[16,48,256]{2,1,0:T(8,128)(2,1)S(1)} all-to-all(bf16[16,48,256]{2,1,0:T(8,128)(2,1)S(1)} %get-tuple-element.26), channel_id=1, replica_groups=mesh['y'=4,'core'=2,'x'=4,'z'=16] {'z'}, dimensions={0} | all-to-all | bytes 786432 | tf_op jit(solution)/shard_map/all_to_all | solution.py:240
  95.7 1.0 softmax.1
  96.7 7.7 %all-to-all-start.3 = ((bf16[16,48,256]{2,1,0:T(8,128)(2,1)}), bf16[16,48,256]{2,1,0:T(8,128)(2,1)S(1)}, u32[]{:S(2)}, u32[]{:S(2)}) async-start(bf16[16,48,256]{2,1,0:T(8,128)(2,1)} %softmax.1), calls=%async_computation.3 | async-start | bytes 786432 | tf_op jit(solution)/shard_map/all_to_all | solution.py:248
  104.4 4.9 %collective-permute-start.6 = (bf16[512,128]{1,0:T(8,128)(2,1)S(1)}, bf16[512,128]{1,0:T(8,128)(2,1)S(1)}, u32[]{:S(2)}, u32[]{:S(2)}) collective-permute-start(bf16[512,128]{1,0:T(8,128)(2,1)S(1)} %get-tuple-element.29), channel_id=1, source_target_pairs={{0,256},{128,384},{256,0},{384,128},{1,257},{129,385},{257,1},{385... | collective-permute-start | bytes 393224 | tf_op jit(solution)/shard_map/ppermute | solution.py:193
  109.3 3.0 %collective-permute-start.5 = (bf16[512,128]{1,0:T(8,128)(2,1)S(1)}, bf16[512,128]{1,0:T(8,128)(2,1)S(1)}, u32[]{:S(2)}, u32[]{:S(2)}) collective-permute-start(bf16[512,128]{1,0:T(8,128)(2,1)S(1)} %get-tuple-element.29), channel_id=1, source_target_pairs={{0,384},{128,0},{256,128},{384,256},{1,385},{129,1},{257,129},{385... | collective-permute-start | bytes 393224 | tf_op jit(solution)/shard_map/ppermute | solution.py:193
  112.3 2.9 %collective-permute-start.4 = (bf16[512,128]{1,0:T(8,128)(2,1)S(1)}, bf16[512,128]{1,0:T(8,128)(2,1)S(1)}, u32[]{:S(2)}, u32[]{:S(2)}) collective-permute-start(bf16[512,128]{1,0:T(8,128)(2,1)S(1)} %get-tuple-element.29), channel_id=1, source_target_pairs={{0,128},{128,256},{256,384},{384,0},{1,129},{129,257},{257,385},{3... | collective-permute-start | bytes 393224 | tf_op jit(solution)/shard_map/ppermute | solution.py:193
  115.2 1.0 collective-permute-done.5
  116.2 4.2 %collective-permute-done.4 = bf16[512,128]{1,0:T(8,128)(2,1)S(1)} collective-permute-done((bf16[512,128]{1,0:T(8,128)(2,1)S(1)}, bf16[512,128]{1,0:T(8,128)(2,1)S(1)}, u32[]{:S(2)}, u32[]{:S(2)}) %collective-permute-start.4) | collective-permute-done | bytes 131104 | tf_op jit(solution)/shard_map/ppermute | solution.py:193
  120.4 2.1 %collective-permute-start.7 = (bf16[4,512,128]{2,1,0:T(8,128)(2,1)S(1)}, bf16[4,512,128]{2,1,0:T(8,128)(2,1)S(1)}, u32[]{:S(2)}, u32[]{:S(2)}) collective-permute-start(bf16[4,512,128]{2,1,0:T(8,128)(2,1)S(1)} %pad_maximum_fusion.own_b), channel_id=1, source_target_pairs={{0,64},{64,0},{1,65},{65,1},{2,66},{66,2},{3,67},{67,3},{4,68},{68... | collective-permute-start | bytes 1572872 | tf_op jit(solution)/shard_map/ppermute | solution.py:193
  122.5 1.9 %collective-permute-done.7.other_b = bf16[4,512,128]{2,1,0:T(8,128)(2,1)S(1)} collective-permute-done((bf16[4,512,128]{2,1,0:T(8,128)(2,1)S(1)}, bf16[4,512,128]{2,1,0:T(8,128)(2,1)S(1)}, u32[]{:S(2)}, u32[]{:S(2)}) %collective-permute-start.7) | collective-permute-done | bytes 524320 | tf_op jit(solution)/shard_map/ppermute | solution.py:193
  125.3 1.3 all-to-all-done.3.p_ref
  127.0 14.2 %all_to_all.26.c_ref = bf16[4,256,384]{2,1,0:T(8,128)(2,1)S(1)} all-to-all(bf16[4,256,384]{2,1,0:T(8,128)(2,1)S(1)} %context.1), channel_id=1, replica_groups=mesh['y'=4,'core'=2,'x'=4,'z'=16] {'x'}, dimensions={0} | all-to-all | bytes 1572864 | tf_op jit(solution)/shard_map/all_to_all | solution.py:251
  141.2 1.6 %mix.1 = bf16[2,256,768]{2,1,0:T(8,128)(2,1)} custom-call(s32[1]{0:T(128)S(6)} %copy.8.tally, bf16[4,256,384]{2,1,0:T(8,128)(2,1)S(1)} %all_to_all.26.c_ref, bf16[768,768]{1,0:T(8,128)(2,1)S(1)} %unpack_out.1.w_ref), custom_call_target="tpu_custom_call" | custom-call | flops 1073741824 | bytes 1048576 | tf_op jit(solution)/shard_map/mix/pallas_call | solution.py:253
  (15 shorter events, 4.0 us)
Async XLA Ops:
  3.3 26.2 %collective-permute-start = (bf16[512,768]{1,0:T(8,128)(2,1)}, bf16[512,768]{1,0:T(8,128)(2,1)S(1)}, u32[]{:S(2)}, u32[]{:S(2)}) collective-permute-start(bf16[512,768]{1,0:T(8,128)(2,1)} %get-tuple-element.21.x0), channel_id=1, source_target_pairs={{0,16},{16,32},{32,48},{48,0},{1,17},{17,33},{33,49},{49,1},{2,18}... | collective-permute-start | bytes 2359304 | tf_op jit(solution)/shard_map/ppermute | solution.py:193
  6.7 38.0 %all-to-all-start = ((bf16[64,16,128]{2,1,0:T(8,128)(2,1)}), bf16[64,16,128]{2,1,0:T(8,128)(2,1)S(1)}, u32[]{:S(2)}, u32[]{:S(2)}) async-start(bf16[64,16,128]{2,1,0:T(8,128)(2,1)} %get-tuple-element.19), calls=%async_computation | async-start | bytes 524288 | tf_op jit(solution)/shard_map/all_to_all | solution.py:211
  24.7 25.4 %collective-permute-start.1 = (bf16[512,768]{1,0:T(8,128)(2,1)}, bf16[512,768]{1,0:T(8,128)(2,1)S(1)}, u32[]{:S(2)}, u32[]{:S(2)}) collective-permute-start(bf16[512,768]{1,0:T(8,128)(2,1)} %get-tuple-element.21.x0), channel_id=1, source_target_pairs={{0,48},{16,0},{32,16},{48,32},{1,49},{17,1},{33,17},{49,33},{2,50}... | collective-permute-start | bytes 2359304 | tf_op jit(solution)/shard_map/ppermute | solution.py:193
  29.5 29.0 %collective-permute-start.2 = (bf16[512,768]{1,0:T(8,128)(2,1)S(1)}, bf16[512,768]{1,0:T(8,128)(2,1)}, u32[]{:S(2)}, u32[]{:S(2)}) collective-permute-start(bf16[512,768]{1,0:T(8,128)(2,1)S(1)} %collective-permute-done.x1), channel_id=1, source_target_pairs={{0,16},{16,32},{32,48},{48,0},{1,17},{17,33},{33,49},{49,1},{2,18}... | collective-permute-start | bytes 2359304 | tf_op jit(solution)/shard_map/ppermute | solution.py:193
  45.6 12.9 %all-to-all-start.1 = ((bf16[4,64,8,128]{3,2,1,0:T(8,128)(2,1)}), bf16[4,64,8,128]{3,2,1,0:T(8,128)(2,1)S(1)}, u32[]{:S(2)}, u32[]{:S(2)}) async-start(bf16[4,64,8,128]{3,2,1,0:T(8,128)(2,1)} %get-tuple-element.22), calls=%async_computation.1 | async-start | bytes 1048576 | tf_op jit(solution)/shard_map/all_to_all | solution.py:221
  50.1 13.1 %copy-start = (bf16[512,768]{1,0:T(8,128)(2,1)S(1)}, bf16[512,768]{1,0:T(8,128)(2,1)}, u32[]{:S(2)}) copy-start(bf16[512,768]{1,0:T(8,128)(2,1)} %get-tuple-element.21.x0) | copy-start | bytes 2359300
  58.5 3.8 %collective-permute-start.3 = (bf16[4,64,8,128]{3,2,1,0:T(8,128)(2,1)S(1)}, bf16[4,64,8,128]{3,2,1,0:T(8,128)(2,1)S(1)}, u32[]{:S(2)}, u32[]{:S(2)}) collective-permute-start(bf16[4,64,8,128]{3,2,1,0:T(8,128)(2,1)S(1)} %all-to-all-done.1), channel_id=1, source_target_pairs={{0,64},{64,0},{1,65},{65,1},{2,66},{66,2},{3,67},{67,3},{4,68},{68... | collective-permute-start | bytes 1572872 | tf_op jit(solution)/shard_map/ppermute | solution.py:193
  67.1 0.9 copy-start.1
  96.7 29.9 %all-to-all-start.3 = ((bf16[16,48,256]{2,1,0:T(8,128)(2,1)}), bf16[16,48,256]{2,1,0:T(8,128)(2,1)S(1)}, u32[]{:S(2)}, u32[]{:S(2)}) async-start(bf16[16,48,256]{2,1,0:T(8,128)(2,1)} %softmax.1), calls=%async_computation.3 | async-start | bytes 786432 | tf_op jit(solution)/shard_map/all_to_all | solution.py:248
  104.4 10.8 %collective-permute-start.6 = (bf16[512,128]{1,0:T(8,128)(2,1)S(1)}, bf16[512,128]{1,0:T(8,128)(2,1)S(1)}, u32[]{:S(2)}, u32[]{:S(2)}) collective-permute-start(bf16[512,128]{1,0:T(8,128)(2,1)S(1)} %get-tuple-element.29), channel_id=1, source_target_pairs={{0,256},{128,384},{256,0},{384,128},{1,257},{129,385},{257,1},{385... | collective-permute-start | bytes 393224 | tf_op jit(solution)/shard_map/ppermute | solution.py:193
  109.3 6.9 %collective-permute-start.5 = (bf16[512,128]{1,0:T(8,128)(2,1)S(1)}, bf16[512,128]{1,0:T(8,128)(2,1)S(1)}, u32[]{:S(2)}, u32[]{:S(2)}) collective-permute-start(bf16[512,128]{1,0:T(8,128)(2,1)S(1)} %get-tuple-element.29), channel_id=1, source_target_pairs={{0,384},{128,0},{256,128},{384,256},{1,385},{129,1},{257,129},{385... | collective-permute-start | bytes 393224 | tf_op jit(solution)/shard_map/ppermute | solution.py:193
  112.3 8.1 %collective-permute-start.4 = (bf16[512,128]{1,0:T(8,128)(2,1)S(1)}, bf16[512,128]{1,0:T(8,128)(2,1)S(1)}, u32[]{:S(2)}, u32[]{:S(2)}) collective-permute-start(bf16[512,128]{1,0:T(8,128)(2,1)S(1)} %get-tuple-element.29), channel_id=1, source_target_pairs={{0,128},{128,256},{256,384},{384,0},{1,129},{129,257},{257,385},{3... | collective-permute-start | bytes 393224 | tf_op jit(solution)/shard_map/ppermute | solution.py:193
  120.4 6.1 %copy-start.2 = (bf16[3,256,512]{2,1,0:T(8,128)(2,1)S(1)}, bf16[3,256,512]{2,1,0:T(8,128)(2,1)}, u32[]{:S(2)}) copy-start(bf16[3,256,512]{2,1,0:T(8,128)(2,1)} %copy-done.1) | copy-start | bytes 2359300
  120.4 3.9 %collective-permute-start.7 = (bf16[4,512,128]{2,1,0:T(8,128)(2,1)S(1)}, bf16[4,512,128]{2,1,0:T(8,128)(2,1)S(1)}, u32[]{:S(2)}, u32[]{:S(2)}) collective-permute-start(bf16[4,512,128]{2,1,0:T(8,128)(2,1)S(1)} %pad_maximum_fusion.own_b), channel_id=1, source_target_pairs={{0,64},{64,0},{1,65},{65,1},{2,66},{66,2},{3,67},{67,3},{4,68},{68... | collective-permute-start | bytes 1572872 | tf_op jit(solution)/shard_map/ppermute | solution.py:193

commit v5 on v4

--- a/solution.py
+++ b/solution.py
@@ -26,6 +26,7 @@
 SMEM = pl.BlockSpec(memory_space=pltpu.SMEM)
 VLIMIT = 24 * 1024 * 1024
 VMOST = 60 * 1024 * 1024
+VROOM = 45000000
 
 
 def call(body, out, ins, scratch=(), flops=0, nbytes=1 << 20, name=None, outs=None, limit=VLIMIT):
@@ -235,6 +236,8 @@
         flops=3 << 30,
         nbytes=1 << 23,
         name="logits",
+        outs=(VMEM, ANY),
+        limit=VROOM,
     )(normed, near, far, across, w_in)
 
     s = lax.all_to_all(s, "z", 0, 0, tiled=True)

time: 143 us -> 143 us (level)
  no operation moved by 1% of the time
where the time goes in v5:
time: 143 us; the launch traced here: 142 us
  starting transfers between devices  55.2 us (39%)
  blocking collectives  41.7 us (29%)
  waiting for transfers between devices  32 us (22%)
  Pallas kernels  12.3 us (9%)
    all_to_all x1, blocking collectives, per_device(): s = lax.all_to_all(s, 'z', 0, 0, tiled=True)  27.5 us
    ppermute x8, starting transfers between devices, per_device(): lax.ppermute(a, axis, [(i, (i + d) % n) for i in range(n)])  24.9 us
    all_to_all x1, starting transfers between devices, per_device(): pieces = lax.all_to_all(pieces, ('x', 'z'), 0, 0, tiled=True)  17.9 us
    all_to_all x1, blocking collectives, per_device(): c = lax.all_to_all(c, 'x', 0, 0, tiled=True)  14.2 us
    all_to_all x1, waiting for transfers between devices, per_device(): pieces = lax.all_to_all(pieces, ('x', 'z'), 0, 0, tiled=True)  13.3 us
    ppermute x8, waiting for transfers between devices, per_device(): lax.ppermute(a, axis, [(i, (i + d) % n) for i in range(n)])  8.93 us
    all_to_all x1, waiting for transfers between devices, per_device(): own = lax.all_to_all(early, 'y', 0, 0, tiled=True)  8.42 us
    all_to_all x1, starting transfers between devices, per_device(): p = lax.all_to_all(p, 'z', 0, 0, tiled=True)  7.91 us
  transfers between devices with their start and end apart: 11, of which 7 were waited for; matrix products, arithmetic and copies ran while one was open for 0% of the time, Pallas kernels for 1%

profile of v5, /device:TPU:32, one launch (start us, length us, event | category | flops | bytes accessed | tf_op | source)
XLA Modules:
  0.0 141.9 jit_solution(6540364471786485065)
XLA Ops:
  0.7 2.7 %first.1 = (bf16[64,16,128]{2,1,0:T(8,128)(2,1)}, bf16[512,768]{1,0:T(8,128)(2,1)}) custom-call(s32[1]{0:T(128)} %bitcast.me, s32[1]{0:T(128)S(6)} %copy.8.tally, bf16[512,768]{1,0:T(8,128)(2,1)} %bitcast.13, f32[768]{0:T(1024)} %g_hbm.1, bf16[12,768]{1,0:T(8,128)(2,1)} %q_hbm.1, bf16[12,768]{1,0:T(8,128)(2,1)} %k_hbm.1, bf16[12,768]{1,0:T(8,128)(2,1)} %v_hbm.1, ...), custom_call_target="tpu_custom_call" | custom-call | bytes 1048576 | tf_op jit(solution)/shard_map/first/pallas_call | solution.py:197
  3.3 3.4 %collective-permute-start = (bf16[512,768]{1,0:T(8,128)(2,1)}, bf16[512,768]{1,0:T(8,128)(2,1)S(1)}, u32[]{:S(2)}, u32[]{:S(2)}) collective-permute-start(bf16[512,768]{1,0:T(8,128)(2,1)} %get-tuple-element.21.x0), channel_id=1, source_target_pairs={{0,16},{16,32},{32,48},{48,0},{1,17},{17,33},{33,49},{49,1},{2,18}... | collective-permute-start | bytes 2359304 | tf_op jit(solution)/shard_map/ppermute | solution.py:194
  6.7 17.9 %all-to-all-start = ((bf16[64,16,128]{2,1,0:T(8,128)(2,1)}), bf16[64,16,128]{2,1,0:T(8,128)(2,1)S(1)}, u32[]{:S(2)}, u32[]{:S(2)}) async-start(bf16[64,16,128]{2,1,0:T(8,128)(2,1)} %get-tuple-element.19), calls=%async_computation | async-start | bytes 524288 | tf_op jit(solution)/shard_map/all_to_all | solution.py:212
  24.7 4.8 %collective-permute-start.1 = (bf16[512,768]{1,0:T(8,128)(2,1)}, bf16[512,768]{1,0:T(8,128)(2,1)S(1)}, u32[]{:S(2)}, u32[]{:S(2)}) collective-permute-start(bf16[512,768]{1,0:T(8,128)(2,1)} %get-tuple-element.21.x0), channel_id=1, source_target_pairs={{0,48},{16,0},{32,16},{48,32},{1,49},{17,1},{33,17},{49,33},{2,50}... | collective-permute-start | bytes 2359304 | tf_op jit(solution)/shard_map/ppermute | solution.py:194
  29.5 1.9 %collective-permute-start.2 = (bf16[512,768]{1,0:T(8,128)(2,1)S(1)}, bf16[512,768]{1,0:T(8,128)(2,1)}, u32[]{:S(2)}, u32[]{:S(2)}) collective-permute-start(bf16[512,768]{1,0:T(8,128)(2,1)S(1)} %collective-permute-done.x1), channel_id=1, source_target_pairs={{0,16},{16,32},{32,48},{48,0},{1,17},{17,33},{33,49},{49,1},{2,18}... | collective-permute-start | bytes 2359304 | tf_op jit(solution)/shard_map/ppermute | solution.py:194
  31.4 13.3 %all-to-all-done.pieces_ref = bf16[64,16,128]{2,1,0:T(8,128)(2,1)S(1)} async-done(((bf16[64,16,128]{2,1,0:T(8,128)(2,1)}), bf16[64,16,128]{2,1,0:T(8,128)(2,1)S(1)}, u32[]{:S(2)}, u32[]{:S(2)}) %all-to-all-start) | async-done | bytes 262176 | tf_op jit(solution)/shard_map/all_to_all | solution.py:212
  45.6 4.5 %all-to-all-start.1 = ((bf16[4,64,8,128]{3,2,1,0:T(8,128)(2,1)}), bf16[4,64,8,128]{3,2,1,0:T(8,128)(2,1)S(1)}, u32[]{:S(2)}, u32[]{:S(2)}) async-start(bf16[4,64,8,128]{3,2,1,0:T(8,128)(2,1)} %get-tuple-element.22), calls=%async_computation.1 | async-start | bytes 1048576 | tf_op jit(solution)/shard_map/all_to_all | solution.py:222
  50.1 8.4 %all-to-all-done.1 = bf16[4,64,8,128]{3,2,1,0:T(8,128)(2,1)S(1)} async-done(((bf16[4,64,8,128]{3,2,1,0:T(8,128)(2,1)}), bf16[4,64,8,128]{3,2,1,0:T(8,128)(2,1)S(1)}, u32[]{:S(2)}, u32[]{:S(2)}) %all-to-all-start.1) | async-done | bytes 524320 | tf_op jit(solution)/shard_map/all_to_all | solution.py:222
  58.5 1.9 %collective-permute-start.3 = (bf16[4,64,8,128]{3,2,1,0:T(8,128)(2,1)S(1)}, bf16[4,64,8,128]{3,2,1,0:T(8,128)(2,1)S(1)}, u32[]{:S(2)}, u32[]{:S(2)}) collective-permute-start(bf16[4,64,8,128]{3,2,1,0:T(8,128)(2,1)S(1)} %all-to-all-done.1), channel_id=1, source_target_pairs={{0,64},{64,0},{1,65},{65,1},{2,66},{66,2},{3,67},{67,3},{4,68},{68... | collective-permute-start | bytes 1572872 | tf_op jit(solution)/shard_map/ppermute | solution.py:194
  60.4 1.9 %collective-permute-done.3 = bf16[4,64,8,128]{3,2,1,0:T(8,128)(2,1)S(1)} collective-permute-done((bf16[4,64,8,128]{3,2,1,0:T(8,128)(2,1)S(1)}, bf16[4,64,8,128]{3,2,1,0:T(8,128)(2,1)S(1)}, u32[]{:S(2)}, u32[]{:S(2)}) %collective-permute-start.3) | collective-permute-done | bytes 524320 | tf_op jit(solution)/shard_map/ppermute | solution.py:194
  63.1 4.0 %logits.1 = (bf16[16,48,256]{2,1,0:T(8,128)(2,1)S(1)}, bf16[3,256,512]{2,1,0:T(8,128)(2,1)S(1)}) custom-call(bf16[512,768]{1,0:T(8,128)(2,1)S(1)} %copy-done, bf16[512,768]{1,0:T(8,128)(2,1)S(1)} %collective-permute-done.x1, bf16[512,768]{1,0:T(8,128)(2,1)S(1)} %collective-permute-done.1.x2, bf16[512,768]{1,0:T(8,128)(2,1)} %collective-permute-done.2.x3, ...), custom_call_target="tpu_custom_call" | custom-call | flops 3221225472 | bytes 8388608 | tf_op jit(solution)/shard_map/logits/pallas_call | solution.py:231
  67.2 27.5 %all_to_all.25.s_ref = bf16[16,48,256]{2,1,0:T(8,128)(2,1)S(1)} all-to-all(bf16[16,48,256]{2,1,0:T(8,128)(2,1)S(1)} %get-tuple-element.26), channel_id=1, replica_groups=mesh['y'=4,'core'=2,'x'=4,'z'=16] {'z'}, dimensions={0} | all-to-all | bytes 786432 | tf_op jit(solution)/shard_map/all_to_all | solution.py:243
  94.6 1.0 softmax.1
  95.6 7.9 %all-to-all-start.3 = ((bf16[16,48,256]{2,1,0:T(8,128)(2,1)}), bf16[16,48,256]{2,1,0:T(8,128)(2,1)S(1)}, u32[]{:S(2)}, u32[]{:S(2)}) async-start(bf16[16,48,256]{2,1,0:T(8,128)(2,1)} %softmax.1), calls=%async_computation.3 | async-start | bytes 786432 | tf_op jit(solution)/shard_map/all_to_all | solution.py:251
  103.5 4.9 %collective-permute-start.6 = (bf16[512,128]{1,0:T(8,128)(2,1)S(1)}, bf16[512,128]{1,0:T(8,128)(2,1)S(1)}, u32[]{:S(2)}, u32[]{:S(2)}) collective-permute-start(bf16[512,128]{1,0:T(8,128)(2,1)S(1)} %get-tuple-element.29), channel_id=1, source_target_pairs={{0,256},{128,384},{256,0},{384,128},{1,257},{129,385},{257,1},{385... | collective-permute-start | bytes 393224 | tf_op jit(solution)/shard_map/ppermute | solution.py:194
  108.5 3.0 %collective-permute-start.5 = (bf16[512,128]{1,0:T(8,128)(2,1)S(1)}, bf16[512,128]{1,0:T(8,128)(2,1)S(1)}, u32[]{:S(2)}, u32[]{:S(2)}) collective-permute-start(bf16[512,128]{1,0:T(8,128)(2,1)S(1)} %get-tuple-element.29), channel_id=1, source_target_pairs={{0,384},{128,0},{256,128},{384,256},{1,385},{129,1},{257,129},{385... | collective-permute-start | bytes 393224 | tf_op jit(solution)/shard_map/ppermute | solution.py:194
  111.5 2.9 %collective-permute-start.4 = (bf16[512,128]{1,0:T(8,128)(2,1)S(1)}, bf16[512,128]{1,0:T(8,128)(2,1)S(1)}, u32[]{:S(2)}, u32[]{:S(2)}) collective-permute-start(bf16[512,128]{1,0:T(8,128)(2,1)S(1)} %get-tuple-element.29), channel_id=1, source_target_pairs={{0,128},{128,256},{256,384},{384,0},{1,129},{129,257},{257,385},{3... | collective-permute-start | bytes 393224 | tf_op jit(solution)/shard_map/ppermute | solution.py:194
  114.3 1.0 collective-permute-done.5
  115.3 4.2 %collective-permute-done.4 = bf16[512,128]{1,0:T(8,128)(2,1)S(1)} collective-permute-done((bf16[512,128]{1,0:T(8,128)(2,1)S(1)}, bf16[512,128]{1,0:T(8,128)(2,1)S(1)}, u32[]{:S(2)}, u32[]{:S(2)}) %collective-permute-start.4) | collective-permute-done | bytes 131104 | tf_op jit(solution)/shard_map/ppermute | solution.py:194
  119.6 2.1 %collective-permute-start.7 = (bf16[4,512,128]{2,1,0:T(8,128)(2,1)S(1)}, bf16[4,512,128]{2,1,0:T(8,128)(2,1)S(1)}, u32[]{:S(2)}, u32[]{:S(2)}) collective-permute-start(bf16[4,512,128]{2,1,0:T(8,128)(2,1)S(1)} %pad_maximum_fusion.own_b), channel_id=1, source_target_pairs={{0,64},{64,0},{1,65},{65,1},{2,66},{66,2},{3,67},{67,3},{4,68},{68... | collective-permute-start | bytes 1572872 | tf_op jit(solution)/shard_map/ppermute | solution.py:194
  121.7 1.9 %collective-permute-done.7.other_b = bf16[4,512,128]{2,1,0:T(8,128)(2,1)S(1)} collective-permute-done((bf16[4,512,128]{2,1,0:T(8,128)(2,1)S(1)}, bf16[4,512,128]{2,1,0:T(8,128)(2,1)S(1)}, u32[]{:S(2)}, u32[]{:S(2)}) %collective-permute-start.7) | collective-permute-done | bytes 524320 | tf_op jit(solution)/shard_map/ppermute | solution.py:194
  124.4 1.3 all-to-all-done.3.p_ref
  126.2 14.2 %all_to_all.26.c_ref = bf16[4,256,384]{2,1,0:T(8,128)(2,1)S(1)} all-to-all(bf16[4,256,384]{2,1,0:T(8,128)(2,1)S(1)} %context.1), channel_id=1, replica_groups=mesh['y'=4,'core'=2,'x'=4,'z'=16] {'x'}, dimensions={0} | all-to-all | bytes 1572864 | tf_op jit(solution)/shard_map/all_to_all | solution.py:254
  140.4 1.6 %mix.1 = bf16[2,256,768]{2,1,0:T(8,128)(2,1)} custom-call(s32[1]{0:T(128)S(6)} %copy.8.tally, bf16[4,256,384]{2,1,0:T(8,128)(2,1)S(1)} %all_to_all.26.c_ref, bf16[768,768]{1,0:T(8,128)(2,1)S(1)} %unpack_out.1.w_ref), custom_call_target="tpu_custom_call" | custom-call | flops 1073741824 | bytes 1048576 | tf_op jit(solution)/shard_map/mix/pallas_call | solution.py:256
  (15 shorter events, 3.1 us)
Async XLA Ops:
  3.3 26.2 %collective-permute-start = (bf16[512,768]{1,0:T(8,128)(2,1)}, bf16[512,768]{1,0:T(8,128)(2,1)S(1)}, u32[]{:S(2)}, u32[]{:S(2)}) collective-permute-start(bf16[512,768]{1,0:T(8,128)(2,1)} %get-tuple-element.21.x0), channel_id=1, source_target_pairs={{0,16},{16,32},{32,48},{48,0},{1,17},{17,33},{33,49},{49,1},{2,18}... | collective-permute-start | bytes 2359304 | tf_op jit(solution)/shard_map/ppermute | solution.py:194
  6.7 38.0 %all-to-all-start = ((bf16[64,16,128]{2,1,0:T(8,128)(2,1)}), bf16[64,16,128]{2,1,0:T(8,128)(2,1)S(1)}, u32[]{:S(2)}, u32[]{:S(2)}) async-start(bf16[64,16,128]{2,1,0:T(8,128)(2,1)} %get-tuple-element.19), calls=%async_computation | async-start | bytes 524288 | tf_op jit(solution)/shard_map/all_to_all | solution.py:212
  24.7 25.4 %collective-permute-start.1 = (bf16[512,768]{1,0:T(8,128)(2,1)}, bf16[512,768]{1,0:T(8,128)(2,1)S(1)}, u32[]{:S(2)}, u32[]{:S(2)}) collective-permute-start(bf16[512,768]{1,0:T(8,128)(2,1)} %get-tuple-element.21.x0), channel_id=1, source_target_pairs={{0,48},{16,0},{32,16},{48,32},{1,49},{17,1},{33,17},{49,33},{2,50}... | collective-permute-start | bytes 2359304 | tf_op jit(solution)/shard_map/ppermute | solution.py:194
  29.5 29.0 %collective-permute-start.2 = (bf16[512,768]{1,0:T(8,128)(2,1)S(1)}, bf16[512,768]{1,0:T(8,128)(2,1)}, u32[]{:S(2)}, u32[]{:S(2)}) collective-permute-start(bf16[512,768]{1,0:T(8,128)(2,1)S(1)} %collective-permute-done.x1), channel_id=1, source_target_pairs={{0,16},{16,32},{32,48},{48,0},{1,17},{17,33},{33,49},{49,1},{2,18}... | collective-permute-start | bytes 2359304 | tf_op jit(solution)/shard_map/ppermute | solution.py:194
  45.6 12.9 %all-to-all-start.1 = ((bf16[4,64,8,128]{3,2,1,0:T(8,128)(2,1)}), bf16[4,64,8,128]{3,2,1,0:T(8,128)(2,1)S(1)}, u32[]{:S(2)}, u32[]{:S(2)}) async-start(bf16[4,64,8,128]{3,2,1,0:T(8,128)(2,1)} %get-tuple-element.22), calls=%async_computation.1 | async-start | bytes 1048576 | tf_op jit(solution)/shard_map/all_to_all | solution.py:222
  50.1 13.1 %copy-start = (bf16[512,768]{1,0:T(8,128)(2,1)S(1)}, bf16[512,768]{1,0:T(8,128)(2,1)}, u32[]{:S(2)}) copy-start(bf16[512,768]{1,0:T(8,128)(2,1)} %get-tuple-element.21.x0) | copy-start | bytes 2359300
  58.5 3.8 %collective-permute-start.3 = (bf16[4,64,8,128]{3,2,1,0:T(8,128)(2,1)S(1)}, bf16[4,64,8,128]{3,2,1,0:T(8,128)(2,1)S(1)}, u32[]{:S(2)}, u32[]{:S(2)}) collective-permute-start(bf16[4,64,8,128]{3,2,1,0:T(8,128)(2,1)S(1)} %all-to-all-done.1), channel_id=1, source_target_pairs={{0,64},{64,0},{1,65},{65,1},{2,66},{66,2},{3,67},{67,3},{4,68},{68... | collective-permute-start | bytes 1572872 | tf_op jit(solution)/shard_map/ppermute | solution.py:194
  67.1 28.5 %copy-start.1 = (bf16[3,256,512]{2,1,0:T(8,128)(2,1)}, bf16[3,256,512]{2,1,0:T(8,128)(2,1)S(1)}, u32[]{:S(2)}) copy-start(bf16[3,256,512]{2,1,0:T(8,128)(2,1)S(1)} %get-tuple-element.31.v_ref) | copy-start | bytes 2359300
  95.6 30.1 %all-to-all-start.3 = ((bf16[16,48,256]{2,1,0:T(8,128)(2,1)}), bf16[16,48,256]{2,1,0:T(8,128)(2,1)S(1)}, u32[]{:S(2)}, u32[]{:S(2)}) async-start(bf16[16,48,256]{2,1,0:T(8,128)(2,1)} %softmax.1), calls=%async_computation.3 | async-start | bytes 786432 | tf_op jit(solution)/shard_map/all_to_all | solution.py:251
  103.5 10.8 %collective-permute-start.6 = (bf16[512,128]{1,0:T(8,128)(2,1)S(1)}, bf16[512,128]{1,0:T(8,128)(2,1)S(1)}, u32[]{:S(2)}, u32[]{:S(2)}) collective-permute-start(bf16[512,128]{1,0:T(8,128)(2,1)S(1)} %get-tuple-element.29), channel_id=1, source_target_pairs={{0,256},{128,384},{256,0},{384,128},{1,257},{129,385},{257,1},{385... | collective-permute-start | bytes 393224 | tf_op jit(solution)/shard_map/ppermute | solution.py:194
  108.5 6.9 %collective-permute-start.5 = (bf16[512,128]{1,0:T(8,128)(2,1)S(1)}, bf16[512,128]{1,0:T(8,128)(2,1)S(1)}, u32[]{:S(2)}, u32[]{:S(2)}) collective-permute-start(bf16[512,128]{1,0:T(8,128)(2,1)S(1)} %get-tuple-element.29), channel_id=1, source_target_pairs={{0,384},{128,0},{256,128},{384,256},{1,385},{129,1},{257,129},{385... | collective-permute-start | bytes 393224 | tf_op jit(solution)/shard_map/ppermute | solution.py:194
  111.5 8.1 %collective-permute-start.4 = (bf16[512,128]{1,0:T(8,128)(2,1)S(1)}, bf16[512,128]{1,0:T(8,128)(2,1)S(1)}, u32[]{:S(2)}, u32[]{:S(2)}) collective-permute-start(bf16[512,128]{1,0:T(8,128)(2,1)S(1)} %get-tuple-element.29), channel_id=1, source_target_pairs={{0,128},{128,256},{256,384},{384,0},{1,129},{129,257},{257,385},{3... | collective-permute-start | bytes 393224 | tf_op jit(solution)/shard_map/ppermute | solution.py:194
  119.6 6.1 %copy-start.2 = (bf16[3,256,512]{2,1,0:T(8,128)(2,1)S(1)}, bf16[3,256,512]{2,1,0:T(8,128)(2,1)}, u32[]{:S(2)}) copy-start(bf16[3,256,512]{2,1,0:T(8,128)(2,1)} %copy-done.1) | copy-start | bytes 2359300
  119.6 3.9 %collective-permute-start.7 = (bf16[4,512,128]{2,1,0:T(8,128)(2,1)S(1)}, bf16[4,512,128]{2,1,0:T(8,128)(2,1)S(1)}, u32[]{:S(2)}, u32[]{:S(2)}) collective-permute-start(bf16[4,512,128]{2,1,0:T(8,128)(2,1)S(1)} %pad_maximum_fusion.own_b), channel_id=1, source_target_pairs={{0,64},{64,0},{1,65},{65,1},{2,66},{66,2},{3,67},{67,3},{4,68},{68... | collective-permute-start | bytes 1572872 | tf_op jit(solution)/shard_map/ppermute | solution.py:194
